TPU v7x, 512 devices: a whole 4x8x8 slice. The times are simulated.
512 devices in a mesh: group: 32 (over x, z), section: 2 (over core), tensor: 8 (over y).
Axes of the slice: x: 4, y: 8, z: 8, core: 2. Of those that a mesh axis runs over, the one named last changes fastest.
Arguments:
- queries: bfloat16 [2, 64, 4096], P('section', 'group', 'tensor'), may hold values from -100 to 100, as said below
- kv_cache: bfloat16 [2, 64, 2, 512, 1024], P('section', 'group', None, None, 'tensor'), may hold values from -20 to 20, as said below
- new_kv: bfloat16 [2, 64, 2, 1024], P('section', 'group', None, 'tensor'), may hold values from -6 to 6
- residual: bfloat16 [2, 64, 4096], P('section', 'group', 'tensor'), may hold values from -6 to 6
- out_weight: bfloat16 [2, 4096, 4096], P('section', 'tensor'), may hold values from -0.5 to 0.5
- dest_cell: int32 [64], replicated, may hold values from 0 to 127, as said below
- lengths: int32 [64], replicated, may hold values from 1 to 511
Outputs:
- handed: bfloat16 [2, 128, 4096], P('section', 'group', 'tensor')
- migrated_cache: bfloat16 [2, 128, 2, 512, 1024], P('section', 'group', None, None, 'tensor')
Inputs may be any that keep to these rules, and one draw needn't show every extreme that they name: queries lie within the stated bounds. `kv_cache`: cache entries lie within the stated bounds. `dest_cell`: entries are distinct; dest_cell[r] // 4 is the group that row r moves to, and rows r with the same r // 2 start in the same group. Half of the groups receive exactly 4 rows each, the others none; the rows of one group go to distinct groups.
All inputs are finite; a program needn't handle non-finite values.
Results may differ from a plain program's by a relative error of at most 0.008.
Values may be sent and summed in bfloat16 or wider, within the bound.
A program may use at most 64 MiB of HBM per device.

v0:
```python
import jax
import jax.numpy as jnp
from jax import lax
from jax.sharding import PartitionSpec as P

HD = 128


NEG_FILL = -1e30


def passed_along(shard, axis, by):
    count = lax.axis_size(axis)
    return lax.ppermute(shard, axis, [(i, (i + by) % count) for i in range(count)])


def attend(query_rows, cache_rows, fresh_rows, valid_counts, kv_heads):
    n_rows = query_rows.shape[0]
    positions = cache_rows.shape[2]
    head_dim = HD
    group_ratio = query_rows.shape[-1] // (kv_heads * head_dim)
    score_scale = 1.0 / head_dim**0.5
    query_heads = query_rows.reshape(n_rows, kv_heads, group_ratio, head_dim)
    keys_all = cache_rows[:, 0].reshape(n_rows, positions, kv_heads, head_dim)
    values_all = cache_rows[:, 1].reshape(n_rows, positions, kv_heads, head_dim)
    fresh_key = fresh_rows[:, 0].reshape(n_rows, kv_heads, head_dim)
    fresh_value = fresh_rows[:, 1].astype(jnp.float32).reshape(n_rows, kv_heads, head_dim)
    scores = (
        jnp.einsum("ngrd,npgd->ngrp", query_heads, keys_all, preferred_element_type=jnp.float32)
        * score_scale
    )
    own_score = (
        jnp.einsum("ngrd,ngd->ngr", query_heads, fresh_key, preferred_element_type=jnp.float32)
        * score_scale
    )
    valid = (jnp.arange(positions, dtype=jnp.int32)[None, :] < valid_counts[:, None])[
        :, None, None, :
    ]
    masked = jnp.where(valid, scores, NEG_FILL)
    row_top = jnp.maximum(jnp.max(masked, axis=-1), own_score)
    exp_scores = jnp.where(valid, jnp.exp(masked - row_top[..., None]), 0.0)
    own_exp = jnp.exp(own_score - row_top)
    denominator = jnp.sum(exp_scores, axis=-1) + own_exp
    weights = (exp_scores / denominator[..., None]).astype(jnp.bfloat16)
    own_weight = (own_exp / denominator).astype(jnp.bfloat16)
    mixed = jnp.einsum("ngrp,npgd->ngrd", weights, values_all, preferred_element_type=jnp.float32)
    mixed = mixed + own_weight.astype(jnp.float32)[..., None] * fresh_value[:, :, None, :]
    return mixed.reshape(n_rows, -1).astype(jnp.bfloat16)


def append_token(cache_rows, fresh_rows, valid_counts):
    positions = cache_rows.shape[2]
    at_end = jnp.arange(positions, dtype=jnp.int32)[None, :] == valid_counts[:, None]
    return jnp.where(at_end[:, None, :, None], fresh_rows[:, :, None, :], cache_rows)


def shards(queries, kv_cache, new_kv, residual, out_weight, dest_cell, lengths):
    groups = lax.axis_size("group")
    my_group = lax.axis_index("group")
    local_rows = queries.shape[1]
    capacity = 2 * local_rows
    kv_local = kv_cache.shape[-1] // HD
    my_cells = lax.dynamic_slice_in_dim(dest_cell, my_group * local_rows, local_rows)
    targets = my_cells // capacity
    match_send = targets[None, :] == jnp.arange(groups, dtype=jnp.int32)[:, None]
    send_row = jnp.sum(
        jnp.where(match_send, jnp.arange(local_rows, dtype=jnp.int32)[None, :], 0), axis=1
    )
    send_live = jnp.any(match_send, axis=1)
    cell_table = dest_cell.reshape(groups, local_rows)
    slot_ids = my_group * capacity + jnp.arange(capacity, dtype=jnp.int32)
    match_recv = cell_table[:, :, None] == slot_ids[None, None, :]
    source_of = jnp.sum(
        jnp.where(match_recv, jnp.arange(groups, dtype=jnp.int32)[:, None, None], 0), axis=(0, 1)
    )
    slot_counts = jnp.sum(
        jnp.where(match_recv, lengths.reshape(groups, local_rows)[:, :, None], 0), axis=(0, 1)
    )
    filled = jnp.any(match_recv, axis=(0, 1))

    def pack_rows(array):
        picked = jnp.take(array, send_row, axis=0)
        live_mask = send_live.reshape((groups,) + (1,) * (array.ndim - 1))
        return jnp.where(live_mask, picked, jnp.zeros_like(picked))

    def take_slots(array):
        return jnp.take(array, source_of, axis=0)

    got_query, got_cache, got_fresh, got_carry = (
        lax.all_to_all(pack_rows(queries[0]), "group", split_axis=0, concat_axis=0, tiled=True),
        lax.all_to_all(pack_rows(kv_cache[0]), "group", split_axis=0, concat_axis=0, tiled=True),
        lax.all_to_all(pack_rows(new_kv[0]), "group", split_axis=0, concat_axis=0, tiled=True),
        lax.all_to_all(pack_rows(residual[0]), "group", split_axis=0, concat_axis=0, tiled=True),
    )
    slot_cache = take_slots(got_cache)
    slot_fresh = take_slots(got_fresh)
    attended = attend(take_slots(got_query), slot_cache, slot_fresh, slot_counts, kv_local)
    moved_cache = append_token(slot_cache, slot_fresh, slot_counts)
    carried = take_slots(got_carry)
    moved_cache = jnp.where(filled[:, None, None, None], moved_cache, jnp.zeros_like(moved_cache))
    projected = jnp.dot(attended, out_weight[0], preferred_element_type=jnp.float32)
    summed = lax.psum(projected, "tensor")
    share_width = residual.shape[-1]
    own_share = lax.dynamic_slice_in_dim(
        summed, lax.axis_index("tensor") * share_width, share_width, 1
    )
    result = jnp.where(filled[:, None], carried.astype(jnp.float32) + own_share, 0.0).astype(
        jnp.bfloat16
    )
    handed = passed_along(result[None], "section", 1)
    return (handed, moved_cache[None])


def solution(mesh):
    in_specs = (
        P("section", "group", "tensor"),
        P("section", "group", None, None, "tensor"),
        P("section", "group", None, "tensor"),
        P("section", "group", "tensor"),
        P("section", "tensor", None),
        P(),
        P(),
    )
    out_specs = (P("section", "group", "tensor"), P("section", "group", None, None, "tensor"))
    return jax.shard_map(shards, mesh=mesh, in_specs=in_specs, out_specs=out_specs, check_vma=False)
```

profile of v0, /device:TPU:1, one launch (start us, length us, event | category | flops | bytes accessed | tf_op | source)
XLA Modules:
  0.0 355.1 jit_solution(10131037596078834958)
XLA Ops:
  7.2 0.8 and_select_fusion
  8.2 1.3 gather_fusion.2
  9.5 0.7 broadcast_select_fusion.1
  10.2 13.7 %all-to-all-start.3 = ((bf16[32,2,128]{2,1,0:T(2,128)(2,1)}), bf16[32,2,128]{2,1,0:T(2,128)(2,1)S(1)}, u32[]{:S(2)}, u32[]{:S(2)}) async-start(bf16[32,2,128]{2,1,0:T(2,128)(2,1)} %broadcast_select_fusion.1), calls=%async_computation.3 | async-start | bytes 32768 | tf_op jit(solution)/shard_map/all_to_all | solution.py:92
  23.9 1.3 gather_fusion.4
  25.3 1.3 gather_fusion.6
  26.7 4.7 %gather_fusion = bf16[32,2,512,128]{3,2,1,0:T(8,128)(2,1)} fusion(bf16[2,2,512,128]{3,2,1,0:T(8,128)(2,1)S(1)} %bitcast.54, s32[1024]{0:T(1024)S(1)} %pad_clamp_fusion.1), kind=kCustom, calls=%fused_computation.4 | custom fusion | bytes 16777344 | tf_op jit(solution)/shard_map/jit(_take)/gather | solution.py:82
  31.9 0.7 reduce.4
  32.6 0.6 reshape.278
  33.2 9.2 %all-to-all-start.1 = ((bf16[32,2,256]{2,1,0:T(2,128)(2,1)}), bf16[32,2,256]{2,1,0:T(2,128)(2,1)S(1)}, u32[]{:S(2)}, u32[]{:S(2)}) async-start(bf16[32,2,256]{2,1,0:T(2,128)(2,1)} %reshape.278), calls=%async_computation.1 | async-start | bytes 65536 | tf_op jit(solution)/shard_map/all_to_all | solution.py:90
  42.5 7.6 %select_select_fusion = bf16[32,2,512,128]{3,2,1,0:T(8,128)(2,1)} fusion(bf16[32,2,512,128]{3,2,1,0:T(8,128)(2,1)} %gather_fusion, pred[32]{0:T(512)(128)(4,1)S(1)} %compare_and_fusion.1, pred[32]{0:T(512)(128)(4,1)S(1)} %fusion.20), kind=kLoop, calls=%fused_computation.8 | loop fusion | flops 8388608 | bytes 16777280 | tf_op jit(solution)/shard_map/jit(_where)/select_n | solution.py:84
  50.0 1.2 all-to-all-done.1
  51.2 8.3 %all-to-all-start.2 = ((bf16[32,2,512,128]{3,2,1,0:T(8,128)(2,1)}), bf16[32,2,512,128]{3,2,1,0:T(8,128)(2,1)}, u32[]{:S(2)}, u32[]{:S(2)}) async-start(bf16[32,2,512,128]{3,2,1,0:T(8,128)(2,1)} %select_select_fusion), calls=%async_computation.2 | async-start | bytes 16777216 | tf_op jit(solution)/shard_map/all_to_all | solution.py:91
  59.9 0.7 reduce.5
  60.6 0.6 reshape.280
  63.0 180.2 %all-to-all-done.2 = bf16[32,2,512,128]{3,2,1,0:T(8,128)(2,1)} async-done(((bf16[32,2,512,128]{3,2,1,0:T(8,128)(2,1)}), bf16[32,2,512,128]{3,2,1,0:T(8,128)(2,1)}, u32[]{:S(2)}, u32[]{:S(2)}) %all-to-all-start.2) | async-done | bytes 8388640 | tf_op jit(solution)/shard_map/all_to_all | solution.py:91
  243.2 13.1 %all-to-all-start = ((bf16[32,2,256]{2,1,0:T(2,128)(2,1)}), bf16[32,2,256]{2,1,0:T(2,128)(2,1)S(1)}, u32[]{:S(2)}, u32[]{:S(2)}) async-start(bf16[32,2,256]{2,1,0:T(2,128)(2,1)} %reshape.280), calls=%async_computation | async-start | bytes 65536 | tf_op jit(solution)/shard_map/all_to_all | solution.py:93
  256.4 4.1 %gather_fusion.1 = bf16[4,2,512,128]{3,2,1,0:T(8,128)(2,1)S(1)} fusion(bf16[32,2,512,128]{3,2,1,0:T(8,128)(2,1)} %all-to-all-done.2, s32[1024]{0:T(1024)S(1)} %pad_clamp_fusion), kind=kCustom, calls=%fused_computation.5 | custom fusion | bytes 2097168 | tf_op jit(solution)/shard_map/jit(_take)/gather | solution.py:87
  261.5 3.5 fusion
  265.8 72.4 %all-reduce.2.cloned.1.call-done = f32[4,4096]{1,0:T(4,128)} async-done(((f32[4,4096]{1,0:T(4,128)}), f32[4,4096]{1,0:T(4,128)}) %all-reduce.2.cloned.1.call-update) | async-done | bytes 65552 | tf_op jit(solution)/shard_map/psum | solution.py:102
  338.2 0.8 fusion.16
  338.9 7.4 %collective-permute-start = (bf16[1,4,512]{2,1,0:T(4,128)(2,1)S(1)}, bf16[1,4,512]{2,1,0:T(4,128)(2,1)S(1)}, u32[]{:S(2)}, u32[]{:S(2)}) collective-permute-start(bf16[1,4,512]{2,1,0:T(4,128)(2,1)S(1)} %fusion.16), channel_id=1, source_target_pairs={{0,8},{8,0},{1,9},{9,1},{2,10},{10,2},{3,11},{11,3},{4,12},{12,4},... | collective-permute-start | bytes 12296 | tf_op jit(solution)/shard_map/ppermute | solution.py:14
  346.4 1.3 fusion.6
  347.6 0.6 copy.41
  (51 shorter events, 4.7 us)
Async XLA Ops:
  7.2 19.5 %copy-start = (bf16[1,2,2,512,128]{4,3,2,1,0:T(8,128)(2,1)S(1)}, bf16[1,2,2,512,128]{4,3,2,1,0:T(8,128)(2,1)}, u32[]{:S(2)}) copy-start(bf16[1,2,2,512,128]{4,3,2,1,0:T(8,128)(2,1)} %param.12) | copy-start | bytes 1572868
  10.2 23.0 %all-to-all-start.3 = ((bf16[32,2,128]{2,1,0:T(2,128)(2,1)}), bf16[32,2,128]{2,1,0:T(2,128)(2,1)S(1)}, u32[]{:S(2)}, u32[]{:S(2)}) async-start(bf16[32,2,128]{2,1,0:T(2,128)(2,1)} %broadcast_select_fusion.1), calls=%async_computation.3 | async-start | bytes 32768 | tf_op jit(solution)/shard_map/all_to_all | solution.py:92
  33.2 18.0 %all-to-all-start.1 = ((bf16[32,2,256]{2,1,0:T(2,128)(2,1)}), bf16[32,2,256]{2,1,0:T(2,128)(2,1)S(1)}, u32[]{:S(2)}, u32[]{:S(2)}) async-start(bf16[32,2,256]{2,1,0:T(2,128)(2,1)} %reshape.278), calls=%async_computation.1 | async-start | bytes 65536 | tf_op jit(solution)/shard_map/all_to_all | solution.py:90
  50.0 9.5 %copy-start.1 = (s32[64]{0:T(128)S(1)}, s32[64]{0:T(128)}, u32[]{:S(2)}) copy-start(s32[64]{0:T(128)} %param.16) | copy-start | bytes 772
  50.0 9.6 %copy-start.2 = (s32[64]{0:T(128)S(1)}, s32[64]{0:T(128)}, u32[]{:S(2)}) copy-start(s32[64]{0:T(128)} %param.17) | copy-start | bytes 772
  51.2 192.0 %all-to-all-start.2 = ((bf16[32,2,512,128]{3,2,1,0:T(8,128)(2,1)}), bf16[32,2,512,128]{3,2,1,0:T(8,128)(2,1)}, u32[]{:S(2)}, u32[]{:S(2)}) async-start(bf16[32,2,512,128]{3,2,1,0:T(8,128)(2,1)} %select_select_fusion), calls=%async_computation.2 | async-start | bytes 16777216 | tf_op jit(solution)/shard_map/all_to_all | solution.py:91
  243.2 22.0 %all-to-all-start = ((bf16[32,2,256]{2,1,0:T(2,128)(2,1)}), bf16[32,2,256]{2,1,0:T(2,128)(2,1)S(1)}, u32[]{:S(2)}, u32[]{:S(2)}) async-start(bf16[32,2,256]{2,1,0:T(2,128)(2,1)} %reshape.280), calls=%async_computation | async-start | bytes 65536 | tf_op jit(solution)/shard_map/all_to_all | solution.py:93
  256.3 81.8 %all-reduce.2.cloned.1.call-start = ((), (), s32[]{:S(2)}) async-start(), calls=%async_computation.4 | async-start | bytes 131072 | tf_op jit(solution)/shard_map/psum | solution.py:102
  338.9 8.7 %collective-permute-start = (bf16[1,4,512]{2,1,0:T(4,128)(2,1)S(1)}, bf16[1,4,512]{2,1,0:T(4,128)(2,1)S(1)}, u32[]{:S(2)}, u32[]{:S(2)}) collective-permute-start(bf16[1,4,512]{2,1,0:T(4,128)(2,1)S(1)} %fusion.16), channel_id=1, source_target_pairs={{0,8},{8,0},{1,9},{9,1},{2,10},{10,2},{3,11},{11,3},{4,12},{12,4},... | collective-permute-start | bytes 12296 | tf_op jit(solution)/shard_map/ppermute | solution.py:14
Sparse Core Ops, SparseCore 0:
  265.1 73.0 all-reduce.1
where the time goes:
time: 356 us; the launch traced here: 355 us
  waiting for transfers between devices  254 us (71%)
  starting transfers between devices  51.8 us (15%)
  local copies, waits for them, and re-layouts  17.3 us (5%)
  between operations  14.3 us (4%)
  other arithmetic  13.8 us (4%)
  matrix products  4.18 us (1%)
    all_to_all x1, waiting for transfers between devices, shards(): lax.all_to_all(pack_rows(kv_cache[0]), 'group', split_axis=0, concat_axis...  180 us
    psum x1, waiting for transfers between devices, shards(): summed = lax.psum(projected, 'tensor')  72.4 us
    all_to_all x1, starting transfers between devices, shards(): lax.all_to_all(pack_rows(new_kv[0]), 'group', split_axis=0, concat_axis=0...  13.7 us
    all_to_all x1, starting transfers between devices, shards(): lax.all_to_all(pack_rows(residual[0]), 'group', split_axis=0, concat_axis...  13.1 us
    all_to_all x1, starting transfers between devices, shards(): lax.all_to_all(pack_rows(queries[0]), 'group', split_axis=0, concat_axis=...  9.23 us
    gather x4, local copies, waits for them, and re-layouts, pack_rows(): picked = jnp.take(array, send_row, axis=0)  8.66 us
    select_n x2, other arithmetic, pack_rows(): return jnp.where(live_mask, picked, jnp.zeros_like(picked))  8.31 us
    all_to_all x1, starting transfers between devices, shards(): lax.all_to_all(pack_rows(kv_cache[0]), 'group', split_axis=0, concat_axis...  8.31 us
  transfers between devices with their start and end apart: 6, of which 3 were waited for; matrix products, arithmetic and copies ran while one was open for 9% of the time, Pallas kernels for 0%

commit v1 on v0

v1 whole, which is shorter than its diff:
```python
import functools

import jax
import jax.numpy as jnp
from jax import lax
from jax.experimental import pallas as pl
from jax.experimental.pallas import tpu as pltpu
from jax.sharding import PartitionSpec as P

HD = 128
NZ = 8
MESH = pl.DeviceIdType.MESH


def move_kernel(
    nx, nz, nt,
    dest_hbm, len_hbm, q_hbm, kv_hbm, fresh_hbm, res_hbm, w_hbm,
    handed_ref, cache_ref,
    dest_ref, len_ref, q_ref, fresh_ref, res_ref, row_of, row_of_ref,
    kv, w, got_k, got_v, put_k, put_v, part, red, lay_own, lay,
    in_sem, small_sem, row_sem, w_sem, own_sem, sent_sem, k1_sem, v1_sem, k2_sem, v2_sem, red_sent, red_sem, layz_sent, layx_sent, layz_sem, layx_sem,
):
    groups = nx * nz
    ctx = kv.shape[2]
    span = ctx // groups
    rows = 2 * groups
    g = lax.axis_index("group")
    s = lax.axis_index("section")
    t = lax.axis_index("tensor")
    x = g // nz
    z = g % nz

    load_kv = pltpu.make_async_copy(kv_hbm.at[0], kv, in_sem)
    load_kv.start()
    small = [
        pltpu.make_async_copy(src, dst, small_sem.at[i])
        for i, (src, dst) in enumerate(
            ((len_hbm, len_ref), (fresh_hbm, fresh_ref), (q_hbm, q_ref), (dest_hbm, dest_ref), (res_hbm, res_ref))
        )
    ]
    for load in small:
        load.start()

    barrier = pltpu.get_barrier_semaphore()

    def greet_group(k, carry):
        pl.semaphore_signal(barrier, inc=1, device_id={"group": (g + k) % groups}, device_id_type=MESH)
        return carry

    def greet_tensor(k, carry):
        pl.semaphore_signal(barrier, inc=1, device_id={"tensor": (t + k) % nt}, device_id_type=MESH)
        return carry

    def greet_section(k, carry):
        pl.semaphore_signal(
            barrier, inc=1, device_id={"group": x * nz + (z + k) % nz, "section": 1 - s}, device_id_type=MESH
        )
        return carry

    lax.fori_loop(1, groups, greet_group, 0)
    lax.fori_loop(1, nt, greet_tensor, 0)
    lax.fori_loop(0, nz, greet_section, 0)

    for load in small:
        load.wait()
    len0 = len_ref[2 * g]
    len1 = len_ref[2 * g + 1]
    load_kv.wait()
    load_w = pltpu.make_async_copy(w_hbm.at[0], w, w_sem)
    load_w.start()
    pos = lax.broadcasted_iota(jnp.int32, (ctx, HD), 0)
    for r, n in ((0, len0), (1, len1)):
        here = pos == n
        for c in range(2):
            token = jnp.broadcast_to(fresh_ref[0, r, c : c + 1, :].astype(jnp.float32), (ctx, HD))
            kv[r, c] = jnp.where(here, token, kv[r, c].astype(jnp.float32)).astype(jnp.bfloat16)
    zero = jnp.zeros((span, HD), jnp.bfloat16)
    got_k[rows] = zero
    got_v[rows] = zero
    mine = pl.ds(pl.multiple_of(span * g, span), span)
    for r in range(2):
        got_k[2 * g + r] = kv[r, 0, mine, :]
        got_v[2 * g + r] = kv[r, 1, mine, :]

    pl.semaphore_wait(barrier, groups - 1 + nt - 1 + nz)

    def partner(k):
        i = k + jnp.where(k >= 1, 1, 0)
        far = nz // 2 - i // (2 * nx)
        dx = (i // 2) % nx
        dz = jnp.where(i % 2 == 0, far, jnp.where(far == nz // 2, 0, nz - far))
        return ((x + dx) % nx) * nz + (z + dz) % nz

    def hop1(c, dst, sem):
        def send(k, carry):
            d = partner(k)
            pltpu.make_async_remote_copy(
                src_ref=kv.at[:, c, pl.ds(pl.multiple_of(span * d, span), span), :],
                dst_ref=dst.at[pl.ds(2 * g, 2)],
                send_sem=sent_sem.at[c],
                recv_sem=sem,
                device_id={"group": d},
                device_id_type=MESH,
            ).start()
            return carry

        lax.fori_loop(0, groups - 1, send, 0)

    hop1(0, got_k, k1_sem)
    hop1(1, got_v, v1_sem)

    cells = row_of.shape[1]
    cell = lax.broadcasted_iota(jnp.int32, (8, cells), 1)

    def place(r, found):
        return jnp.where(cell == dest_ref[r], r, found)

    found = lax.fori_loop(0, rows, place, jnp.full((8, cells), rows, jnp.int32), unroll=8)
    row_of[...] = found
    load_row_of = pltpu.make_async_copy(row_of, row_of_ref, row_sem)
    load_row_of.start()

    qf = q_ref[0].astype(jnp.float32)
    q8 = jnp.concatenate(
        [qf[r : r + 1, h * HD : (h + 1) * HD] for r in range(2) for h in range(4)], axis=0
    ).astype(jnp.bfloat16)
    dims = (((1,), (1,)), ((), ()))
    first = lax.broadcasted_iota(jnp.int32, (8, ctx), 0) < 4
    scores = jnp.where(
        first,
        lax.dot_general(q8, kv[0, 0], dims, preferred_element_type=jnp.float32),
        lax.dot_general(q8, kv[1, 0], dims, preferred_element_type=jnp.float32),
    ) * (1.0 / HD**0.5)
    valid = lax.broadcasted_iota(jnp.int32, (8, ctx), 1) <= jnp.where(first, len0, len1)
    scores = jnp.where(valid, scores, -1e30)
    top = jnp.max(scores, axis=1, keepdims=True)
    e = jnp.where(valid, jnp.exp(scores - top), 0.0)
    weights = (e / jnp.sum(e, axis=1, keepdims=True)).astype(jnp.bfloat16)
    sub = lax.broadcasted_iota(jnp.int32, (8, HD), 0)
    attended = jnp.where(
        sub < 4,
        jnp.dot(weights, kv[0, 1], preferred_element_type=jnp.float32),
        jnp.dot(weights, kv[1, 1], preferred_element_type=jnp.float32),
    )
    lhs = jnp.concatenate(
        [jnp.where(sub % 4 == h, attended, 0.0) for h in range(4)], axis=1
    ).astype(jnp.bfloat16)

    def wait_bytes(ref, sem):
        pltpu.make_async_copy(ref, ref, sem).wait()

    def hop2(c, got, put, sem, own):
        def copy_slots(d):
            for slot in range(4):
                put[4 * d + slot] = got[row_of_ref[0, 4 * d + slot]]

        def send(k, carry):
            d = partner(k)
            copy_slots(d)
            pltpu.make_async_remote_copy(
                src_ref=put.at[pl.ds(4 * d, 4)],
                dst_ref=cache_ref.at[0, :, c, mine, :],
                send_sem=sent_sem.at[2 + c],
                recv_sem=sem,
                device_id={"group": d},
                device_id_type=MESH,
            ).start()
            return carry

        lax.fori_loop(0, groups - 1, send, 0)
        copy_slots(g)
        pltpu.make_async_copy(put.at[pl.ds(4 * g, 4)], cache_ref.at[0, :, c, mine, :], own).start()

    load_row_of.wait()
    wait_bytes(got_k.at[pl.ds(0, rows - 2)], k1_sem)
    hop2(0, got_k, put_k, k2_sem, own_sem.at[0])

    width = res_ref.shape[2]
    load_w.wait()

    def project(k, carry):
        d = (t + k) % nt
        cols = pl.ds(pl.multiple_of(width * d, width), width)
        p8 = jnp.dot(lhs, w[:, cols], preferred_element_type=jnp.float32)
        both = jnp.concatenate(
            [jnp.sum(p8[0:4], axis=0, keepdims=True), jnp.sum(p8[4:8], axis=0, keepdims=True)], axis=0
        )
        part[d] = both

        @pl.when(k < nt)
        def _():
            pltpu.make_async_remote_copy(
                src_ref=part.at[d],
                dst_ref=red.at[t],
                send_sem=red_sent,
                recv_sem=red_sem,
                device_id={"tensor": d},
                device_id_type=MESH,
            ).start()

        return carry

    lax.fori_loop(1, nt + 1, project, 0)
    red[t] = part[t]

    wait_bytes(got_v.at[pl.ds(0, rows - 2)], v1_sem)
    hop2(1, got_v, put_v, v2_sem, own_sem.at[1])

    wait_bytes(red.at[pl.ds(0, nt - 1)], red_sem)
    total = red[0]
    for i in range(1, nt):
        total = total + red[i]
    total = total + res_ref[0].astype(jnp.float32)
    lay_own[0] = total[0:1]
    lay_own[1] = total[1:2]

    def hand(k, carry):
        pltpu.make_async_remote_copy(
            src_ref=lay_own,
            dst_ref=lay.at[pl.ds(2 * g, 2)],
            send_sem=layz_sent,
            recv_sem=layz_sem,
            device_id={"group": x * nz + (z + k) % nz, "section": 1 - s},
            device_id_type=MESH,
        ).start()
        return carry

    lax.fori_loop(0, nz, hand, 0)

    ring = pl.ds(2 * nz * x, 2 * nz)
    wait_bytes(lay.at[pl.ds(0, 2 * nz)], layz_sem)

    def spread(k, carry):
        pltpu.make_async_remote_copy(
            src_ref=lay.at[ring],
            dst_ref=lay.at[ring],
            send_sem=layx_sent,
            recv_sem=layx_sem,
            device_id={"group": ((x + k) % nx) * nz + z},
            device_id_type=MESH,
        ).start()
        return carry

    lax.fori_loop(1, nx, spread, 0)
    wait_bytes(lay.at[pl.ds(0, 2 * nz * (nx - 1))], layx_sem)
    out_rows = []
    for slot in range(4):
        r = row_of_ref[0, 4 * g + slot]
        out_rows.append(jnp.where(r < rows, lay[jnp.minimum(r, rows - 1)], 0.0))
    handed_ref[0] = jnp.concatenate(out_rows, axis=0).astype(jnp.bfloat16)

    wait_bytes(part.at[pl.ds(0, nt - 1)], red_sent)
    wait_bytes(lay.at[pl.ds(0, 2 * nz)], layz_sent)
    wait_bytes(lay.at[pl.ds(0, 2 * nz * (nx - 1))], layx_sent)
    wait_bytes(got_k.at[pl.ds(0, rows - 2)], sent_sem.at[0])
    wait_bytes(got_v.at[pl.ds(0, rows - 2)], sent_sem.at[1])
    for c, put, sem in ((0, put_k, k2_sem), (1, put_v, v2_sem)):
        pltpu.make_async_copy(put.at[pl.ds(4 * g, 4)], cache_ref.at[0, :, c, mine, :], own_sem.at[c]).wait()
        wait_bytes(put.at[pl.ds(0, 4 * (groups - 1))], sent_sem.at[2 + c])
        wait_bytes(put.at[pl.ds(0, 4 * (groups - 1))], sem)


def write_kernel(handed, moved, handed_hbm, moved_hbm, sem):
    copies = [pltpu.make_async_copy(moved.at[0, i], moved_hbm.at[0, i], sem.at[i]) for i in range(4)]
    copies.append(pltpu.make_async_copy(handed, handed_hbm, sem.at[4]))
    for copy in copies:
        copy.start()
    for copy in copies:
        copy.wait()


def shards(nx, nz, nt, queries, kv_cache, new_kv, residual, out_weight, dest_cell, lengths):
    groups = nx * nz
    rows = 2 * groups
    cells = 4 * groups
    ctx = kv_cache.shape[3]
    span = ctx // groups
    width = residual.shape[-1]
    bf = jnp.bfloat16
    f32 = jnp.float32
    dma = pltpu.SemaphoreType.DMA
    vmem = pl.BlockSpec(memory_space=pltpu.VMEM)
    hbm = pl.BlockSpec(memory_space=pltpu.HBM)
    handed, moved = pl.pallas_call(
        functools.partial(move_kernel, nx, nz, nt),
        out_shape=(pltpu.VMEM((1, 4, width), bf), pltpu.VMEM((1, 4, 2, ctx, HD), bf)),
        in_specs=[hbm] * 7,
        out_specs=(vmem, vmem),
        scratch_shapes=[
            pltpu.SMEM((rows,), jnp.int32),
            pltpu.SMEM((rows,), jnp.int32),
            pltpu.VMEM(queries.shape, bf),
            pltpu.VMEM(new_kv.shape, bf),
            pltpu.VMEM(residual.shape, bf),
            pltpu.VMEM((8, cells), jnp.int32),
            pltpu.SMEM((8, cells), jnp.int32),
            pltpu.VMEM((2, 2, ctx, HD), bf),
            pltpu.VMEM(out_weight.shape[1:], bf),
            pltpu.VMEM((rows + 1, span, HD), bf),
            pltpu.VMEM((rows + 1, span, HD), bf),
            pltpu.VMEM((cells, span, HD), bf),
            pltpu.VMEM((cells, span, HD), bf),
            pltpu.VMEM((nt, 2, width), f32),
            pltpu.VMEM((nt, 2, width), f32),
            pltpu.VMEM((2, 1, width), f32),
            pltpu.VMEM((rows, 1, width), f32),
            dma, dma((5,)), dma, dma, dma((2,)), dma((4,)), dma, dma, dma, dma, dma, dma, dma, dma, dma, dma,
        ],
        compiler_params=pltpu.CompilerParams(
            collective_id=0, has_side_effects=True, vmem_limit_bytes=60 * 1024 * 1024
        ),
    )(dest_cell, lengths, queries, kv_cache, new_kv, residual, out_weight)
    return pl.pallas_call(
        write_kernel,
        out_shape=(
            jax.ShapeDtypeStruct(handed.shape, bf),
            jax.ShapeDtypeStruct(moved.shape, bf),
        ),
        in_specs=[vmem, vmem],
        out_specs=(hbm, hbm),
        scratch_shapes=[dma((5,))],
    )(handed, moved)


def solution(mesh):
    in_specs = (
        P("section", "group", "tensor"),
        P("section", "group", None, None, "tensor"),
        P("section", "group", None, "tensor"),
        P("section", "group", "tensor"),
        P("section", "tensor", None),
        P(),
        P(),
    )
    out_specs = (P("section", "group", "tensor"), P("section", "group", None, None, "tensor"))
    nz = min(NZ, mesh.shape["group"] // 2)
    body = functools.partial(shards, mesh.shape["group"] // nz, nz, mesh.shape["tensor"])
    return jax.shard_map(body, mesh=mesh, in_specs=in_specs, out_specs=out_specs, check_vma=False)
```

time: 356 us -> 61.2 us (0.17)
  waiting for transfers between devices: 254 us -> 0 us
  Pallas kernels: 0 us -> 58.8 us
  starting transfers between devices: 51.8 us -> 0 us
  local copies, waits for them, and re-layouts: 17.3 us -> 1.56 us
  other arithmetic: 13.8 us -> 0 us
  between operations: 14.3 us -> 0.65 us
  matrix products: 4.18 us -> 0 us
    all_to_all x4 -> x0, waiting for transfers between devices: 181 us -> none  [the longest x1 180 us: shards(): lax.all_to_all(pack_rows(kv_cache[0]), 'group', split_axis=0, concat_axis...]
    psum x1 -> x0, waiting for transfers between devices: 72.4 us -> none  [shards(): summed = lax.psum(projected, 'tensor')]
    pallas_call x0 -> x2, Pallas kernels: none -> 58.8 us  [the longest x1 56.6 us: shards(): pl.pallas_call(functools.partial(move_kernel, nx, nz, nt), out_shape=(plt...]
    all_to_all x4 -> x0, starting transfers between devices: 44.4 us -> none  [the longest x1 13.7 us: shards(): lax.all_to_all(pack_rows(new_kv[0]), 'group', split_axis=0, concat_axis=0...]
    gather x8 -> x0, local copies, waits for them, and re-layouts: 14.5 us -> none  [the longest x4 8.66 us: pack_rows(): picked = jnp.take(array, send_row, axis=0)]
    select_n x11 -> x0, other arithmetic: 10.7 us -> none  [the longest x2 8.31 us: pack_rows(): return jnp.where(live_mask, picked, jnp.zeros_like(picked))]
    ppermute x1 -> x0, starting transfers between devices: 7.41 us -> none  [passed_along(): lax.ppermute(shard, axis, [(i, (i + by) % count) for i in range(count)])]
    dot_general x4 -> x0, matrix products: 4.18 us -> none  [the longest x1 3.49 us: shards(): jnp.dot(attended, out_weight[0], preferred_element_type=jnp.float32)]
  transfers between devices with their start and end apart: 6 -> 0, of which waited for: 3 -> 0; matrix products, arithmetic and copies ran while one was open for 9% -> 0% of each run, Pallas kernels for 0% -> 0%
where the time goes in v1:
time: 61.2 us; the launch traced here: 61 us
  Pallas kernels  58.8 us (96%)
  local copies, waits for them, and re-layouts  1.56 us (3%)
  between operations  0.65 us (1%)
    pallas_call x1, Pallas kernels, shards(): pl.pallas_call(functools.partial(move_kernel, nx, nz, nt), out_shape=(plt...  56.6 us
    pallas_call x1, Pallas kernels, shards(): pl.pallas_call(write_kernel, out_shape=(jax.ShapeDtypeStruct(handed.shape...  2.23 us
    unnamed x4, local copies, waits for them, and re-layouts  1.56 us

profile of v1, /device:TPU:1, one launch (start us, length us, event | category | flops | bytes accessed | tf_op | source)
XLA Modules:
  0.0 61.0 jit_solution(1434967878460482018)
XLA Ops:
  0.6 56.6 %shard_map.86 = (bf16[1,4,512]{2,1,0:T(4,128)(2,1)S(1)}, bf16[1,4,2,512,128]{4,3,2,1,0:T(8,128)(2,1)S(1)}) custom-call(s32[64]{0:T(128)} %dest_hbm.1, s32[64]{0:T(128)} %len_hbm.1, bf16[1,2,512]{2,1,0:T(2,128)(2,1)} %q_hbm.1, bf16[1,2,2,512,128]{4,3,2,1,0:T(8,128)(2,1)} %kv_hbm.1, bf16[1,2,2,128]{3,2,1,0:T(2,128)(2,1)} %fresh_hbm.1, ...), custom_call_target="tpu_custom_call" | custom-call | tf_op jit(solution)/shard_map/pallas_call | solution.py:284
  57.2 0.0 copy-start
  57.2 1.0 %copy-done = bf16[1,4,2,512,128]{4,3,2,1,0:T(8,128)(2,1)} copy-done((bf16[1,4,2,512,128]{4,3,2,1,0:T(8,128)(2,1)}, bf16[1,4,2,512,128]{4,3,2,1,0:T(8,128)(2,1)S(1)}, u32[]{:S(2)}) %copy-start) | copy-done | bytes 1048600
  58.2 0.0 copy-start.1
  58.2 0.6 copy-done.1
  58.8 2.2 %shard_map.87 = (bf16[1,4,512]{2,1,0:T(4,128)(2,1)}, bf16[1,4,2,512,128]{4,3,2,1,0:T(8,128)(2,1)}) custom-call(bf16[1,4,512]{2,1,0:T(4,128)(2,1)} %copy-done.1, bf16[1,4,2,512,128]{4,3,2,1,0:T(8,128)(2,1)} %copy-done), custom_call_target="tpu_custom_call" | custom-call | tf_op jit(solution)/shard_map/pallas_call | solution.py:313
Async XLA Ops:
  57.2 1.0 %copy-start = (bf16[1,4,2,512,128]{4,3,2,1,0:T(8,128)(2,1)}, bf16[1,4,2,512,128]{4,3,2,1,0:T(8,128)(2,1)S(1)}, u32[]{:S(2)}) copy-start(bf16[1,4,2,512,128]{4,3,2,1,0:T(8,128)(2,1)S(1)} %get-tuple-element.5.moved) | copy-start | bytes 3145732
  58.2 0.6 copy-start.1

commit v2 on v1

--- a/solution.py
+++ b/solution.py
@@ -91,7 +91,7 @@
         dz = jnp.where(i % 2 == 0, far, jnp.where(far == nz // 2, 0, nz - far))
         return ((x + dx) % nx) * nz + (z + dz) % nz
 
-    def hop1(c, dst, sem):
+    def hop1(c, dst, sem, low, high):
         def send(k, carry):
             d = partner(k)
             pltpu.make_async_remote_copy(
@@ -104,10 +104,9 @@
             ).start()
             return carry
 
-        lax.fori_loop(0, groups - 1, send, 0)
-
-    hop1(0, got_k, k1_sem)
-    hop1(1, got_v, v1_sem)
+        lax.fori_loop(low, high, send, 0)
+
+    hop1(0, got_k, k1_sem, 0, groups - 1)
 
     cells = row_of.shape[1]
     cell = lax.broadcasted_iota(jnp.int32, (8, cells), 1)
@@ -171,9 +170,7 @@
         copy_slots(g)
         pltpu.make_async_copy(put.at[pl.ds(4 * g, 4)], cache_ref.at[0, :, c, mine, :], own).start()
 
-    load_row_of.wait()
-    wait_bytes(got_k.at[pl.ds(0, rows - 2)], k1_sem)
-    hop2(0, got_k, put_k, k2_sem, own_sem.at[0])
+    hop1(1, got_v, v1_sem, 0, groups // 2)
 
     width = res_ref.shape[2]
     load_w.wait()
@@ -203,8 +200,7 @@
     lax.fori_loop(1, nt + 1, project, 0)
     red[t] = part[t]
 
-    wait_bytes(got_v.at[pl.ds(0, rows - 2)], v1_sem)
-    hop2(1, got_v, put_v, v2_sem, own_sem.at[1])
+    hop1(1, got_v, v1_sem, groups // 2, groups - 1)
 
     wait_bytes(red.at[pl.ds(0, nt - 1)], red_sem)
     total = red[0]
@@ -227,6 +223,10 @@
 
     lax.fori_loop(0, nz, hand, 0)
 
+    load_row_of.wait()
+    wait_bytes(got_k.at[pl.ds(0, rows - 2)], k1_sem)
+    hop2(0, got_k, put_k, k2_sem, own_sem.at[0])
+
     ring = pl.ds(2 * nz * x, 2 * nz)
     wait_bytes(lay.at[pl.ds(0, 2 * nz)], layz_sem)
 
@@ -242,6 +242,10 @@
         return carry
 
     lax.fori_loop(1, nx, spread, 0)
+
+    wait_bytes(got_v.at[pl.ds(0, rows - 2)], v1_sem)
+    hop2(1, got_v, put_v, v2_sem, own_sem.at[1])
+
     wait_bytes(lay.at[pl.ds(0, 2 * nz * (nx - 1))], layx_sem)
     out_rows = []
     for slot in range(4):
@@ -319,6 +323,7 @@
         in_specs=[vmem, vmem],
         out_specs=(hbm, hbm),
         scratch_shapes=[dma((5,))],
+        compiler_params=pltpu.CompilerParams(vmem_limit_bytes=8 * 1024 * 1024),
     )(handed, moved)
 
 

time: 61.2 us -> 55.6 us (0.908)
  Pallas kernels: 58.8 us -> 54.8 us
  local copies, waits for them, and re-layouts: 1.56 us -> 0 us
    pallas_call x1, Pallas kernels: 56.6 us -> 53.8 us  [shards(): pl.pallas_call(functools.partial(move_kernel, nx, nz, nt), out_shape=(plt...]
    unnamed x4 -> x0, local copies, waits for them, and re-layouts: 1.56 us -> none
    pallas_call x1, Pallas kernels: 2.23 us -> 1.01 us  [shards(): pl.pallas_call(write_kernel, out_shape=(jax.ShapeDtypeStruct(handed.shape...]
where the time goes in v2:
time: 55.6 us; the launch traced here: 55.4 us
  Pallas kernels  54.8 us (99%)
  between operations  0.64 us (1%)
    pallas_call x1, Pallas kernels, shards(): pl.pallas_call(functools.partial(move_kernel, nx, nz, nt), out_shape=(plt...  53.8 us

profile of v2, /device:TPU:1, one launch (start us, length us, event | category | flops | bytes accessed | tf_op | source)
XLA Modules:
  0.0 55.4 jit_solution(2917160697846274798)
XLA Ops:
  0.6 53.8 %shard_map.86 = (bf16[1,4,512]{2,1,0:T(4,128)(2,1)S(1)}, bf16[1,4,2,512,128]{4,3,2,1,0:T(8,128)(2,1)S(1)}) custom-call(s32[64]{0:T(128)} %dest_hbm.1, s32[64]{0:T(128)} %len_hbm.1, bf16[1,2,512]{2,1,0:T(2,128)(2,1)} %q_hbm.1, bf16[1,2,2,512,128]{4,3,2,1,0:T(8,128)(2,1)} %kv_hbm.1, bf16[1,2,2,128]{3,2,1,0:T(2,128)(2,1)} %fresh_hbm.1, ...), custom_call_target="tpu_custom_call" | custom-call | tf_op jit(solution)/shard_map/pallas_call | solution.py:288
  54.4 1.0 %shard_map.87 = (bf16[1,4,512]{2,1,0:T(4,128)(2,1)}, bf16[1,4,2,512,128]{4,3,2,1,0:T(8,128)(2,1)}) custom-call(bf16[1,4,512]{2,1,0:T(4,128)(2,1)S(1)} %get-tuple-element.4.handed, bf16[1,4,2,512,128]{4,3,2,1,0:T(8,128)(2,1)S(1)} %get-tuple-element.5.moved), custom_call_target="tpu_custom_call" | custom-call | tf_op jit(solution)/shard_map/pallas_call | solution.py:317

commit v3 on v2

--- a/solution.py
+++ b/solution.py
@@ -30,8 +30,9 @@
     x = g // nz
     z = g % nz
 
-    load_kv = pltpu.make_async_copy(kv_hbm.at[0], kv, in_sem)
-    load_kv.start()
+    load_kv = [pltpu.make_async_copy(kv_hbm.at[0, :, c], kv.at[:, c], in_sem.at[c]) for c in range(2)]
+    for load in load_kv:
+        load.start()
     small = [
         pltpu.make_async_copy(src, dst, small_sem.at[i])
         for i, (src, dst) in enumerate(
@@ -65,35 +66,52 @@
         load.wait()
     len0 = len_ref[2 * g]
     len1 = len_ref[2 * g + 1]
-    load_kv.wait()
+    pos = lax.broadcasted_iota(jnp.int32, (ctx, HD), 0)
+    mine = pl.ds(pl.multiple_of(span * g, span), span)
+
+    def append(c, got):
+        load_kv[c].wait()
+        for r, n in ((0, len0), (1, len1)):
+            token = jnp.broadcast_to(fresh_ref[0, r, c : c + 1, :].astype(jnp.float32), (ctx, HD))
+            kv[r, c] = jnp.where(pos == n, token, kv[r, c].astype(jnp.float32)).astype(jnp.bfloat16)
+            got[2 * g + r] = kv[r, c, mine, :]
+        got[rows] = jnp.zeros((span, HD), jnp.bfloat16)
+
+    cells = row_of.shape[1]
+    cell = lax.broadcasted_iota(jnp.int32, (8, cells), 1)
+
+    def place(r, found):
+        return jnp.where(cell == dest_ref[r], r, found)
+
+    found = lax.fori_loop(0, rows, place, jnp.full((8, cells), rows, jnp.int32), unroll=8)
+    row_of[...] = found
+    load_row_of = pltpu.make_async_copy(row_of, row_of_ref, row_sem)
+    load_row_of.start()
+
+    append(0, got_k)
     load_w = pltpu.make_async_copy(w_hbm.at[0], w, w_sem)
     load_w.start()
-    pos = lax.broadcasted_iota(jnp.int32, (ctx, HD), 0)
-    for r, n in ((0, len0), (1, len1)):
-        here = pos == n
-        for c in range(2):
-            token = jnp.broadcast_to(fresh_ref[0, r, c : c + 1, :].astype(jnp.float32), (ctx, HD))
-            kv[r, c] = jnp.where(here, token, kv[r, c].astype(jnp.float32)).astype(jnp.bfloat16)
-    zero = jnp.zeros((span, HD), jnp.bfloat16)
-    got_k[rows] = zero
-    got_v[rows] = zero
-    mine = pl.ds(pl.multiple_of(span * g, span), span)
-    for r in range(2):
-        got_k[2 * g + r] = kv[r, 0, mine, :]
-        got_v[2 * g + r] = kv[r, 1, mine, :]
-
     pl.semaphore_wait(barrier, groups - 1 + nt - 1 + nz)
 
-    def partner(k):
-        i = k + jnp.where(k >= 1, 1, 0)
-        far = nz // 2 - i // (2 * nx)
-        dx = (i // 2) % nx
-        dz = jnp.where(i % 2 == 0, far, jnp.where(far == nz // 2, 0, nz - far))
-        return ((x + dx) % nx) * nz + (z + dz) % nz
+    z_offsets = [o for m in range(nz // 2 - 1, 0, -1) for o in (m, nz - m)]
+    z_offsets[2:2] = [nz // 2]
+    z_offsets.append(0)
+
+    def for_partners(low, high, send):
+        def window(v, carry):
+            for j, dz in enumerate(z_offsets):
+                dx = (j + v) % nx
+                d = ((x + dx) % nx) * nz + (z + dz) % nz
+                if dz == 0:
+                    pl.when(dx != 0)(functools.partial(send, d))
+                else:
+                    send(d)
+            return carry
+
+        lax.fori_loop(low, high, window, 0)
 
     def hop1(c, dst, sem, low, high):
-        def send(k, carry):
-            d = partner(k)
+        def send(d):
             pltpu.make_async_remote_copy(
                 src_ref=kv.at[:, c, pl.ds(pl.multiple_of(span * d, span), span), :],
                 dst_ref=dst.at[pl.ds(2 * g, 2)],
@@ -102,22 +120,11 @@
                 device_id={"group": d},
                 device_id_type=MESH,
             ).start()
-            return carry
-
-        lax.fori_loop(low, high, send, 0)
-
-    hop1(0, got_k, k1_sem, 0, groups - 1)
-
-    cells = row_of.shape[1]
-    cell = lax.broadcasted_iota(jnp.int32, (8, cells), 1)
-
-    def place(r, found):
-        return jnp.where(cell == dest_ref[r], r, found)
-
-    found = lax.fori_loop(0, rows, place, jnp.full((8, cells), rows, jnp.int32), unroll=8)
-    row_of[...] = found
-    load_row_of = pltpu.make_async_copy(row_of, row_of_ref, row_sem)
-    load_row_of.start()
+
+        for_partners(low, high, send)
+
+    hop1(0, got_k, k1_sem, 0, nx)
+    append(1, got_v)
 
     qf = q_ref[0].astype(jnp.float32)
     q8 = jnp.concatenate(
@@ -148,13 +155,12 @@
     def wait_bytes(ref, sem):
         pltpu.make_async_copy(ref, ref, sem).wait()
 
-    def hop2(c, got, put, sem, own):
+    def hop2(c, got, put, sem, low, high):
         def copy_slots(d):
             for slot in range(4):
                 put[4 * d + slot] = got[row_of_ref[0, 4 * d + slot]]
 
-        def send(k, carry):
-            d = partner(k)
+        def send(d):
             copy_slots(d)
             pltpu.make_async_remote_copy(
                 src_ref=put.at[pl.ds(4 * d, 4)],
@@ -164,13 +170,13 @@
                 device_id={"group": d},
                 device_id_type=MESH,
             ).start()
-            return carry
-
-        lax.fori_loop(0, groups - 1, send, 0)
-        copy_slots(g)
-        pltpu.make_async_copy(put.at[pl.ds(4 * g, 4)], cache_ref.at[0, :, c, mine, :], own).start()
-
-    hop1(1, got_v, v1_sem, 0, groups // 2)
+
+        for_partners(low, high, send)
+        if high == nx:
+            copy_slots(g)
+            pltpu.make_async_copy(put.at[pl.ds(4 * g, 4)], cache_ref.at[0, :, c, mine, :], own_sem.at[c]).start()
+
+    hop1(1, got_v, v1_sem, 0, nx // 2)
 
     width = res_ref.shape[2]
     load_w.wait()
@@ -200,7 +206,11 @@
     lax.fori_loop(1, nt + 1, project, 0)
     red[t] = part[t]
 
-    hop1(1, got_v, v1_sem, groups // 2, groups - 1)
+    hop1(1, got_v, v1_sem, nx // 2, nx)
+
+    load_row_of.wait()
+    wait_bytes(got_k.at[pl.ds(0, rows - 2)], k1_sem)
+    hop2(0, got_k, put_k, k2_sem, 0, nx // 2)
 
     wait_bytes(red.at[pl.ds(0, nt - 1)], red_sem)
     total = red[0]
@@ -223,9 +233,7 @@
 
     lax.fori_loop(0, nz, hand, 0)
 
-    load_row_of.wait()
-    wait_bytes(got_k.at[pl.ds(0, rows - 2)], k1_sem)
-    hop2(0, got_k, put_k, k2_sem, own_sem.at[0])
+    hop2(0, got_k, put_k, k2_sem, nx // 2, nx)
 
     ring = pl.ds(2 * nz * x, 2 * nz)
     wait_bytes(lay.at[pl.ds(0, 2 * nz)], layz_sem)
@@ -244,7 +252,7 @@
     lax.fori_loop(1, nx, spread, 0)
 
     wait_bytes(got_v.at[pl.ds(0, rows - 2)], v1_sem)
-    hop2(1, got_v, put_v, v2_sem, own_sem.at[1])
+    hop2(1, got_v, put_v, v2_sem, 0, nx)
 
     wait_bytes(lay.at[pl.ds(0, 2 * nz * (nx - 1))], layx_sem)
     out_rows = []
@@ -308,7 +316,7 @@
             pltpu.VMEM((nt, 2, width), f32),
             pltpu.VMEM((2, 1, width), f32),
             pltpu.VMEM((rows, 1, width), f32),
-            dma, dma((5,)), dma, dma, dma((2,)), dma((4,)), dma, dma, dma, dma, dma, dma, dma, dma, dma, dma,
+            dma((2,)), dma((5,)), dma, dma, dma((2,)), dma((4,)), dma, dma, dma, dma, dma, dma, dma, dma, dma, dma,
         ],
         compiler_params=pltpu.CompilerParams(
             collective_id=0, has_side_effects=True, vmem_limit_bytes=60 * 1024 * 1024

time: 55.6 us -> 55.1 us (level)
  no operation moved by 1% of the time
where the time goes in v3:
time: 55.1 us; the launch traced here: 55 us
  Pallas kernels  54.3 us (99%)
  between operations  0.64 us (1%)
    pallas_call x1, Pallas kernels, shards(): pl.pallas_call(functools.partial(move_kernel, nx, nz, nt), out_shape=(plt...  53.3 us

profile of v3, /device:TPU:1, one launch (start us, length us, event | category | flops | bytes accessed | tf_op | source)
XLA Modules:
  0.0 55.0 jit_solution(9076726673342040352)
XLA Ops:
  0.6 53.3 %shard_map.86 = (bf16[1,4,512]{2,1,0:T(4,128)(2,1)S(1)}, bf16[1,4,2,512,128]{4,3,2,1,0:T(8,128)(2,1)S(1)}) custom-call(s32[64]{0:T(128)} %dest_hbm.1, s32[64]{0:T(128)} %len_hbm.1, bf16[1,2,512]{2,1,0:T(2,128)(2,1)} %q_hbm.1, bf16[1,2,2,512,128]{4,3,2,1,0:T(8,128)(2,1)} %kv_hbm.1, bf16[1,2,2,128]{3,2,1,0:T(2,128)(2,1)} %fresh_hbm.1, ...), custom_call_target="tpu_custom_call" | custom-call | tf_op jit(solution)/shard_map/pallas_call | solution.py:296
  54.0 1.0 %shard_map.87 = (bf16[1,4,512]{2,1,0:T(4,128)(2,1)}, bf16[1,4,2,512,128]{4,3,2,1,0:T(8,128)(2,1)}) custom-call(bf16[1,4,512]{2,1,0:T(4,128)(2,1)S(1)} %get-tuple-element.4.handed, bf16[1,4,2,512,128]{4,3,2,1,0:T(8,128)(2,1)S(1)} %get-tuple-element.5.moved), custom_call_target="tpu_custom_call" | custom-call | tf_op jit(solution)/shard_map/pallas_call | solution.py:325

commit v4 on v3

--- a/solution.py
+++ b/solution.py
@@ -21,8 +21,8 @@
     in_sem, small_sem, row_sem, w_sem, own_sem, sent_sem, k1_sem, v1_sem, k2_sem, v2_sem, red_sent, red_sem, layz_sent, layx_sent, layz_sem, layx_sem,
 ):
     groups = nx * nz
-    ctx = kv.shape[2]
-    span = ctx // groups
+    span = kv.shape[3]
+    ctx = span * groups
     rows = 2 * groups
     g = lax.axis_index("group")
     s = lax.axis_index("section")
@@ -30,9 +30,13 @@
     x = g // nz
     z = g % nz
 
-    load_kv = [pltpu.make_async_copy(kv_hbm.at[0, :, c], kv.at[:, c], in_sem.at[c]) for c in range(2)]
-    for load in load_kv:
-        load.start()
+    load_kv = [
+        [pltpu.make_async_copy(kv_hbm.at[0, r, c], kv.at[c, :, r], in_sem.at[c, r]) for r in range(2)]
+        for c in range(2)
+    ]
+    for c in range(2):
+        for load in load_kv[c]:
+            load.start()
     small = [
         pltpu.make_async_copy(src, dst, small_sem.at[i])
         for i, (src, dst) in enumerate(
@@ -62,31 +66,21 @@
     lax.fori_loop(1, nt, greet_tensor, 0)
     lax.fori_loop(0, nz, greet_section, 0)
 
-    for load in small:
-        load.wait()
+    load_len, load_fresh, *load_rest = small
+    load_len.wait()
+    load_fresh.wait()
     len0 = len_ref[2 * g]
     len1 = len_ref[2 * g + 1]
-    pos = lax.broadcasted_iota(jnp.int32, (ctx, HD), 0)
-    mine = pl.ds(pl.multiple_of(span * g, span), span)
+    chunks = (groups, span, HD)
+    pos = lax.broadcasted_iota(jnp.int32, chunks, 0) * span + lax.broadcasted_iota(jnp.int32, chunks, 1)
 
     def append(c, got):
-        load_kv[c].wait()
         for r, n in ((0, len0), (1, len1)):
-            token = jnp.broadcast_to(fresh_ref[0, r, c : c + 1, :].astype(jnp.float32), (ctx, HD))
-            kv[r, c] = jnp.where(pos == n, token, kv[r, c].astype(jnp.float32)).astype(jnp.bfloat16)
-            got[2 * g + r] = kv[r, c, mine, :]
+            load_kv[c][r].wait()
+            token = jnp.broadcast_to(fresh_ref[0, r, c : c + 1, :].astype(jnp.float32)[None], chunks)
+            kv[c, :, r] = jnp.where(pos == n, token, kv[c, :, r].astype(jnp.float32)).astype(jnp.bfloat16)
+            got[2 * g + r] = kv[c, g, r]
         got[rows] = jnp.zeros((span, HD), jnp.bfloat16)
-
-    cells = row_of.shape[1]
-    cell = lax.broadcasted_iota(jnp.int32, (8, cells), 1)
-
-    def place(r, found):
-        return jnp.where(cell == dest_ref[r], r, found)
-
-    found = lax.fori_loop(0, rows, place, jnp.full((8, cells), rows, jnp.int32), unroll=8)
-    row_of[...] = found
-    load_row_of = pltpu.make_async_copy(row_of, row_of_ref, row_sem)
-    load_row_of.start()
 
     append(0, got_k)
     load_w = pltpu.make_async_copy(w_hbm.at[0], w, w_sem)
@@ -97,11 +91,13 @@
     z_offsets[2:2] = [nz // 2]
     z_offsets.append(0)
 
+    way = 1 - 2 * s
+
     def for_partners(low, high, send):
         def window(v, carry):
             for j, dz in enumerate(z_offsets):
                 dx = (j + v) % nx
-                d = ((x + dx) % nx) * nz + (z + dz) % nz
+                d = ((x + way * dx + nx) % nx) * nz + (z + way * dz + nz) % nz
                 if dz == 0:
                     pl.when(dx != 0)(functools.partial(send, d))
                 else:
@@ -113,7 +109,7 @@
     def hop1(c, dst, sem, low, high):
         def send(d):
             pltpu.make_async_remote_copy(
-                src_ref=kv.at[:, c, pl.ds(pl.multiple_of(span * d, span), span), :],
+                src_ref=kv.at[c, d],
                 dst_ref=dst.at[pl.ds(2 * g, 2)],
                 send_sem=sent_sem.at[c],
                 recv_sem=sem,
@@ -126,16 +122,33 @@
     hop1(0, got_k, k1_sem, 0, nx)
     append(1, got_v)
 
+    for load in load_rest:
+        load.wait()
+    cells = row_of.shape[1]
+    cell = lax.broadcasted_iota(jnp.int32, (8, cells), 1)
+
+    def place(r, found):
+        return jnp.where(cell == dest_ref[r], r, found)
+
+    found = lax.fori_loop(0, rows, place, jnp.full((8, cells), rows, jnp.int32), unroll=8)
+    row_of[...] = found
+    load_row_of = pltpu.make_async_copy(row_of, row_of_ref, row_sem)
+    load_row_of.start()
+
     qf = q_ref[0].astype(jnp.float32)
     q8 = jnp.concatenate(
         [qf[r : r + 1, h * HD : (h + 1) * HD] for r in range(2) for h in range(4)], axis=0
     ).astype(jnp.bfloat16)
     dims = (((1,), (1,)), ((), ()))
+
+    def cached(c, r):
+        return kv[c, :, r].reshape(ctx, HD)
+
     first = lax.broadcasted_iota(jnp.int32, (8, ctx), 0) < 4
     scores = jnp.where(
         first,
-        lax.dot_general(q8, kv[0, 0], dims, preferred_element_type=jnp.float32),
-        lax.dot_general(q8, kv[1, 0], dims, preferred_element_type=jnp.float32),
+        lax.dot_general(q8, cached(0, 0), dims, preferred_element_type=jnp.float32),
+        lax.dot_general(q8, cached(0, 1), dims, preferred_element_type=jnp.float32),
     ) * (1.0 / HD**0.5)
     valid = lax.broadcasted_iota(jnp.int32, (8, ctx), 1) <= jnp.where(first, len0, len1)
     scores = jnp.where(valid, scores, -1e30)
@@ -145,8 +158,8 @@
     sub = lax.broadcasted_iota(jnp.int32, (8, HD), 0)
     attended = jnp.where(
         sub < 4,
-        jnp.dot(weights, kv[0, 1], preferred_element_type=jnp.float32),
-        jnp.dot(weights, kv[1, 1], preferred_element_type=jnp.float32),
+        jnp.dot(weights, cached(1, 0), preferred_element_type=jnp.float32),
+        jnp.dot(weights, cached(1, 1), preferred_element_type=jnp.float32),
     )
     lhs = jnp.concatenate(
         [jnp.where(sub % 4 == h, attended, 0.0) for h in range(4)], axis=1
@@ -164,7 +177,7 @@
             copy_slots(d)
             pltpu.make_async_remote_copy(
                 src_ref=put.at[pl.ds(4 * d, 4)],
-                dst_ref=cache_ref.at[0, :, c, mine, :],
+                dst_ref=cache_ref.at[c, g],
                 send_sem=sent_sem.at[2 + c],
                 recv_sem=sem,
                 device_id={"group": d},
@@ -174,7 +187,7 @@
         for_partners(low, high, send)
         if high == nx:
             copy_slots(g)
-            pltpu.make_async_copy(put.at[pl.ds(4 * g, 4)], cache_ref.at[0, :, c, mine, :], own_sem.at[c]).start()
+            pltpu.make_async_copy(put.at[pl.ds(4 * g, 4)], cache_ref.at[c, g], own_sem.at[c]).start()
 
     hop1(1, got_v, v1_sem, 0, nx // 2)
 
@@ -217,13 +230,12 @@
     for i in range(1, nt):
         total = total + red[i]
     total = total + res_ref[0].astype(jnp.float32)
-    lay_own[0] = total[0:1]
-    lay_own[1] = total[1:2]
+    lay_own[...] = total.astype(jnp.bfloat16)
 
     def hand(k, carry):
         pltpu.make_async_remote_copy(
             src_ref=lay_own,
-            dst_ref=lay.at[pl.ds(2 * g, 2)],
+            dst_ref=lay.at[g],
             send_sem=layz_sent,
             recv_sem=layz_sem,
             device_id={"group": x * nz + (z + k) % nz, "section": 1 - s},
@@ -235,8 +247,8 @@
 
     hop2(0, got_k, put_k, k2_sem, nx // 2, nx)
 
-    ring = pl.ds(2 * nz * x, 2 * nz)
-    wait_bytes(lay.at[pl.ds(0, 2 * nz)], layz_sem)
+    ring = pl.ds(nz * x, nz)
+    wait_bytes(lay.at[pl.ds(0, nz)], layz_sem)
 
     def spread(k, carry):
         pltpu.make_async_remote_copy(
@@ -254,27 +266,32 @@
     wait_bytes(got_v.at[pl.ds(0, rows - 2)], v1_sem)
     hop2(1, got_v, put_v, v2_sem, 0, nx)
 
-    wait_bytes(lay.at[pl.ds(0, 2 * nz * (nx - 1))], layx_sem)
+    wait_bytes(lay.at[pl.ds(0, nz * (nx - 1))], layx_sem)
     out_rows = []
     for slot in range(4):
         r = row_of_ref[0, 4 * g + slot]
-        out_rows.append(jnp.where(r < rows, lay[jnp.minimum(r, rows - 1)], 0.0))
+        both = lay[jnp.minimum(r, rows - 1) // 2].astype(jnp.float32)
+        out_rows.append(jnp.where(r < rows, jnp.where(r % 2 == 0, both[0:1], both[1:2]), 0.0))
     handed_ref[0] = jnp.concatenate(out_rows, axis=0).astype(jnp.bfloat16)
 
     wait_bytes(part.at[pl.ds(0, nt - 1)], red_sent)
-    wait_bytes(lay.at[pl.ds(0, 2 * nz)], layz_sent)
-    wait_bytes(lay.at[pl.ds(0, 2 * nz * (nx - 1))], layx_sent)
+    wait_bytes(lay.at[pl.ds(0, nz)], layz_sent)
+    wait_bytes(lay.at[pl.ds(0, nz * (nx - 1))], layx_sent)
     wait_bytes(got_k.at[pl.ds(0, rows - 2)], sent_sem.at[0])
     wait_bytes(got_v.at[pl.ds(0, rows - 2)], sent_sem.at[1])
     for c, put, sem in ((0, put_k, k2_sem), (1, put_v, v2_sem)):
-        pltpu.make_async_copy(put.at[pl.ds(4 * g, 4)], cache_ref.at[0, :, c, mine, :], own_sem.at[c]).wait()
+        pltpu.make_async_copy(put.at[pl.ds(4 * g, 4)], cache_ref.at[c, g], own_sem.at[c]).wait()
         wait_bytes(put.at[pl.ds(0, 4 * (groups - 1))], sent_sem.at[2 + c])
         wait_bytes(put.at[pl.ds(0, 4 * (groups - 1))], sem)
 
 
 def write_kernel(handed, moved, handed_hbm, moved_hbm, sem):
-    copies = [pltpu.make_async_copy(moved.at[0, i], moved_hbm.at[0, i], sem.at[i]) for i in range(4)]
-    copies.append(pltpu.make_async_copy(handed, handed_hbm, sem.at[4]))
+    copies = [
+        pltpu.make_async_copy(moved.at[c, :, i], moved_hbm.at[0, i, c], sem.at[2 * i + c])
+        for i in range(4)
+        for c in range(2)
+    ]
+    copies.append(pltpu.make_async_copy(handed, handed_hbm, sem.at[8]))
     for copy in copies:
         copy.start()
     for copy in copies:
@@ -295,7 +312,7 @@
     hbm = pl.BlockSpec(memory_space=pltpu.HBM)
     handed, moved = pl.pallas_call(
         functools.partial(move_kernel, nx, nz, nt),
-        out_shape=(pltpu.VMEM((1, 4, width), bf), pltpu.VMEM((1, 4, 2, ctx, HD), bf)),
+        out_shape=(pltpu.VMEM((1, 4, width), bf), pltpu.VMEM((2, groups, 4, span, HD), bf)),
         in_specs=[hbm] * 7,
         out_specs=(vmem, vmem),
         scratch_shapes=[
@@ -306,7 +323,7 @@
             pltpu.VMEM(residual.shape, bf),
             pltpu.VMEM((8, cells), jnp.int32),
             pltpu.SMEM((8, cells), jnp.int32),
-            pltpu.VMEM((2, 2, ctx, HD), bf),
+            pltpu.VMEM((2, groups, 2, span, HD), bf),
             pltpu.VMEM(out_weight.shape[1:], bf),
             pltpu.VMEM((rows + 1, span, HD), bf),
             pltpu.VMEM((rows + 1, span, HD), bf),
@@ -314,25 +331,26 @@
             pltpu.VMEM((cells, span, HD), bf),
             pltpu.VMEM((nt, 2, width), f32),
             pltpu.VMEM((nt, 2, width), f32),
-            pltpu.VMEM((2, 1, width), f32),
-            pltpu.VMEM((rows, 1, width), f32),
-            dma((2,)), dma((5,)), dma, dma, dma((2,)), dma((4,)), dma, dma, dma, dma, dma, dma, dma, dma, dma, dma,
+            pltpu.VMEM((2, width), bf),
+            pltpu.VMEM((groups, 2, width), bf),
+            dma((2, 2)), dma((5,)), dma, dma, dma((2,)), dma((4,)), dma, dma, dma, dma, dma, dma, dma, dma, dma, dma,
         ],
         compiler_params=pltpu.CompilerParams(
             collective_id=0, has_side_effects=True, vmem_limit_bytes=60 * 1024 * 1024
         ),
-    )(dest_cell, lengths, queries, kv_cache, new_kv, residual, out_weight)
-    return pl.pallas_call(
+    )(dest_cell, lengths, queries, kv_cache.reshape(1, 2, 2, groups, span, HD), new_kv, residual, out_weight)
+    handed, moved = pl.pallas_call(
         write_kernel,
         out_shape=(
             jax.ShapeDtypeStruct(handed.shape, bf),
-            jax.ShapeDtypeStruct(moved.shape, bf),
+            jax.ShapeDtypeStruct((1, 4, 2, groups, span, HD), bf),
         ),
         in_specs=[vmem, vmem],
         out_specs=(hbm, hbm),
-        scratch_shapes=[dma((5,))],
+        scratch_shapes=[dma((9,))],
         compiler_params=pltpu.CompilerParams(vmem_limit_bytes=8 * 1024 * 1024),
     )(handed, moved)
+    return handed, moved.reshape(1, 4, 2, ctx, HD)
 
 
 def solution(mesh):

time: 55.1 us -> 54.7 us (level)
  no operation moved by 1% of the time
where the time goes in v4:
time: 54.7 us; the launch traced here: 54.5 us
  Pallas kernels  53.9 us (99%)
  between operations  0.64 us (1%)
    pallas_call x1, Pallas kernels, shards(): pl.pallas_call(functools.partial(move_kernel, nx, nz, nt), out_shape=(plt...  52.9 us

profile of v4, /device:TPU:1, one launch (start us, length us, event | category | flops | bytes accessed | tf_op | source)
XLA Modules:
  0.0 54.5 jit_solution(6874194811431389052)
XLA Ops:
  0.6 52.9 %shard_map.86 = (bf16[1,4,512]{2,1,0:T(4,128)(2,1)S(1)}, bf16[2,32,4,16,128]{4,3,2,1,0:T(8,128)(2,1)S(1)}) custom-call(s32[64]{0:T(128)} %dest_hbm.1, s32[64]{0:T(128)} %len_hbm.1, bf16[1,2,512]{2,1,0:T(2,128)(2,1)} %q_hbm.1, bf16[1,2,2,32,16,128]{5,4,3,2,1,0:T(8,128)(2,1)} %bitcast.2, bf16[1,2,2,128]{3,2,1,0:T(2,128)(2,1)} %fresh_hbm.1, ...), custom_call_target="tpu_custom_call" | custom-call | tf_op jit(solution)/shard_map/pallas_call | solution.py:313
  53.5 1.0 %shard_map.87 = (bf16[1,4,512]{2,1,0:T(4,128)(2,1)}, bf16[1,4,2,32,16,128]{5,4,3,2,1,0:T(8,128)(2,1)}) custom-call(bf16[1,4,512]{2,1,0:T(4,128)(2,1)S(1)} %get-tuple-element.6.handed, bf16[2,32,4,16,128]{4,3,2,1,0:T(8,128)(2,1)S(1)} %get-tuple-element.7.moved), custom_call_target="tpu_custom_call" | custom-call | tf_op jit(solution)/shard_map/pallas_call | solution.py:342

commit v5 on v3

--- a/solution.py
+++ b/solution.py
@@ -27,8 +27,8 @@
     g = lax.axis_index("group")
     s = lax.axis_index("section")
     t = lax.axis_index("tensor")
-    x = g // nz
-    z = g % nz
+    x = lax.div(g, nz)
+    z = lax.rem(g, nz)
 
     load_kv = [pltpu.make_async_copy(kv_hbm.at[0, :, c], kv.at[:, c], in_sem.at[c]) for c in range(2)]
     for load in load_kv:
@@ -45,16 +45,16 @@
     barrier = pltpu.get_barrier_semaphore()
 
     def greet_group(k, carry):
-        pl.semaphore_signal(barrier, inc=1, device_id={"group": (g + k) % groups}, device_id_type=MESH)
+        pl.semaphore_signal(barrier, inc=1, device_id={"group": lax.rem(g + k, groups)}, device_id_type=MESH)
         return carry
 
     def greet_tensor(k, carry):
-        pl.semaphore_signal(barrier, inc=1, device_id={"tensor": (t + k) % nt}, device_id_type=MESH)
+        pl.semaphore_signal(barrier, inc=1, device_id={"tensor": lax.rem(t + k, nt)}, device_id_type=MESH)
         return carry
 
     def greet_section(k, carry):
         pl.semaphore_signal(
-            barrier, inc=1, device_id={"group": x * nz + (z + k) % nz, "section": 1 - s}, device_id_type=MESH
+            barrier, inc=1, device_id={"group": x * nz + lax.rem(z + k, nz), "section": 1 - s}, device_id_type=MESH
         )
         return carry
 
@@ -62,8 +62,9 @@
     lax.fori_loop(1, nt, greet_tensor, 0)
     lax.fori_loop(0, nz, greet_section, 0)
 
-    for load in small:
-        load.wait()
+    load_len, load_fresh, *load_rest = small
+    load_len.wait()
+    load_fresh.wait()
     len0 = len_ref[2 * g]
     len1 = len_ref[2 * g + 1]
     pos = lax.broadcasted_iota(jnp.int32, (ctx, HD), 0)
@@ -77,17 +78,6 @@
             got[2 * g + r] = kv[r, c, mine, :]
         got[rows] = jnp.zeros((span, HD), jnp.bfloat16)
 
-    cells = row_of.shape[1]
-    cell = lax.broadcasted_iota(jnp.int32, (8, cells), 1)
-
-    def place(r, found):
-        return jnp.where(cell == dest_ref[r], r, found)
-
-    found = lax.fori_loop(0, rows, place, jnp.full((8, cells), rows, jnp.int32), unroll=8)
-    row_of[...] = found
-    load_row_of = pltpu.make_async_copy(row_of, row_of_ref, row_sem)
-    load_row_of.start()
-
     append(0, got_k)
     load_w = pltpu.make_async_copy(w_hbm.at[0], w, w_sem)
     load_w.start()
@@ -97,13 +87,16 @@
     z_offsets[2:2] = [nz // 2]
     z_offsets.append(0)
 
+    way = 1 - 2 * s
+
+    z_partners = [lax.rem(z + way * dz + nz, nz) for dz in z_offsets]
+
     def for_partners(low, high, send):
         def window(v, carry):
             for j, dz in enumerate(z_offsets):
-                dx = (j + v) % nx
-                d = ((x + dx) % nx) * nz + (z + dz) % nz
+                d = lax.rem(x + way * (j + v) + nx * nz, nx) * nz + z_partners[j]
                 if dz == 0:
-                    pl.when(dx != 0)(functools.partial(send, d))
+                    pl.when(lax.rem(j + v, nx) != 0)(functools.partial(send, d))
                 else:
                     send(d)
             return carry
@@ -125,6 +118,20 @@
 
     hop1(0, got_k, k1_sem, 0, nx)
     append(1, got_v)
+    hop1(1, got_v, v1_sem, 0, nx)
+
+    for load in load_rest:
+        load.wait()
+    cells = row_of.shape[1]
+    cell = lax.broadcasted_iota(jnp.int32, (8, cells), 1)
+
+    def place(r, found):
+        return jnp.where(cell == dest_ref[r], r, found)
+
+    found = lax.fori_loop(0, rows, place, jnp.full((8, cells), rows, jnp.int32), unroll=8)
+    row_of[...] = found
+    load_row_of = pltpu.make_async_copy(row_of, row_of_ref, row_sem)
+    load_row_of.start()
 
     qf = q_ref[0].astype(jnp.float32)
     q8 = jnp.concatenate(
@@ -176,13 +183,11 @@
             copy_slots(g)
             pltpu.make_async_copy(put.at[pl.ds(4 * g, 4)], cache_ref.at[0, :, c, mine, :], own_sem.at[c]).start()
 
-    hop1(1, got_v, v1_sem, 0, nx // 2)
-
     width = res_ref.shape[2]
     load_w.wait()
 
     def project(k, carry):
-        d = (t + k) % nt
+        d = lax.rem(t + k, nt)
         cols = pl.ds(pl.multiple_of(width * d, width), width)
         p8 = jnp.dot(lhs, w[:, cols], preferred_element_type=jnp.float32)
         both = jnp.concatenate(
@@ -206,8 +211,6 @@
     lax.fori_loop(1, nt + 1, project, 0)
     red[t] = part[t]
 
-    hop1(1, got_v, v1_sem, nx // 2, nx)
-
     load_row_of.wait()
     wait_bytes(got_k.at[pl.ds(0, rows - 2)], k1_sem)
     hop2(0, got_k, put_k, k2_sem, 0, nx // 2)
@@ -217,16 +220,15 @@
     for i in range(1, nt):
         total = total + red[i]
     total = total + res_ref[0].astype(jnp.float32)
-    lay_own[0] = total[0:1]
-    lay_own[1] = total[1:2]
+    lay_own[...] = total.astype(jnp.bfloat16)
 
     def hand(k, carry):
         pltpu.make_async_remote_copy(
             src_ref=lay_own,
-            dst_ref=lay.at[pl.ds(2 * g, 2)],
+            dst_ref=lay.at[g],
             send_sem=layz_sent,
             recv_sem=layz_sem,
-            device_id={"group": x * nz + (z + k) % nz, "section": 1 - s},
+            device_id={"group": x * nz + lax.rem(z + k, nz), "section": 1 - s},
             device_id_type=MESH,
         ).start()
         return carry
@@ -235,8 +237,8 @@
 
     hop2(0, got_k, put_k, k2_sem, nx // 2, nx)
 
-    ring = pl.ds(2 * nz * x, 2 * nz)
-    wait_bytes(lay.at[pl.ds(0, 2 * nz)], layz_sem)
+    ring = pl.ds(nz * x, nz)
+    wait_bytes(lay.at[pl.ds(0, nz)], layz_sem)
 
     def spread(k, carry):
         pltpu.make_async_remote_copy(
@@ -244,7 +246,7 @@
             dst_ref=lay.at[ring],
             send_sem=layx_sent,
             recv_sem=layx_sem,
-            device_id={"group": ((x + k) % nx) * nz + z},
+            device_id={"group": lax.rem(x + k, nx) * nz + z},
             device_id_type=MESH,
         ).start()
         return carry
@@ -254,16 +256,17 @@
     wait_bytes(got_v.at[pl.ds(0, rows - 2)], v1_sem)
     hop2(1, got_v, put_v, v2_sem, 0, nx)
 
-    wait_bytes(lay.at[pl.ds(0, 2 * nz * (nx - 1))], layx_sem)
+    wait_bytes(lay.at[pl.ds(0, nz * (nx - 1))], layx_sem)
     out_rows = []
     for slot in range(4):
         r = row_of_ref[0, 4 * g + slot]
-        out_rows.append(jnp.where(r < rows, lay[jnp.minimum(r, rows - 1)], 0.0))
+        both = lay[jnp.minimum(r, rows - 1) // 2].astype(jnp.float32)
+        out_rows.append(jnp.where(r < rows, jnp.where(r % 2 == 0, both[0:1], both[1:2]), 0.0))
     handed_ref[0] = jnp.concatenate(out_rows, axis=0).astype(jnp.bfloat16)
 
     wait_bytes(part.at[pl.ds(0, nt - 1)], red_sent)
-    wait_bytes(lay.at[pl.ds(0, 2 * nz)], layz_sent)
-    wait_bytes(lay.at[pl.ds(0, 2 * nz * (nx - 1))], layx_sent)
+    wait_bytes(lay.at[pl.ds(0, nz)], layz_sent)
+    wait_bytes(lay.at[pl.ds(0, nz * (nx - 1))], layx_sent)
     wait_bytes(got_k.at[pl.ds(0, rows - 2)], sent_sem.at[0])
     wait_bytes(got_v.at[pl.ds(0, rows - 2)], sent_sem.at[1])
     for c, put, sem in ((0, put_k, k2_sem), (1, put_v, v2_sem)):
@@ -273,8 +276,12 @@
 
 
 def write_kernel(handed, moved, handed_hbm, moved_hbm, sem):
-    copies = [pltpu.make_async_copy(moved.at[0, i], moved_hbm.at[0, i], sem.at[i]) for i in range(4)]
-    copies.append(pltpu.make_async_copy(handed, handed_hbm, sem.at[4]))
+    copies = [
+        pltpu.make_async_copy(moved.at[0, i, c], moved_hbm.at[0, i, c], sem.at[2 * i + c])
+        for i in range(4)
+        for c in range(2)
+    ]
+    copies.append(pltpu.make_async_copy(handed, handed_hbm, sem.at[8]))
     for copy in copies:
         copy.start()
     for copy in copies:
@@ -314,8 +321,8 @@
             pltpu.VMEM((cells, span, HD), bf),
             pltpu.VMEM((nt, 2, width), f32),
             pltpu.VMEM((nt, 2, width), f32),
-            pltpu.VMEM((2, 1, width), f32),
-            pltpu.VMEM((rows, 1, width), f32),
+            pltpu.VMEM((2, width), bf),
+            pltpu.VMEM((groups, 2, width), bf),
             dma((2,)), dma((5,)), dma, dma, dma((2,)), dma((4,)), dma, dma, dma, dma, dma, dma, dma, dma, dma, dma,
         ],
         compiler_params=pltpu.CompilerParams(
@@ -330,7 +337,7 @@
         ),
         in_specs=[vmem, vmem],
         out_specs=(hbm, hbm),
-        scratch_shapes=[dma((5,))],
+        scratch_shapes=[dma((9,))],
         compiler_params=pltpu.CompilerParams(vmem_limit_bytes=8 * 1024 * 1024),
     )(handed, moved)
 

time: 55.1 us -> 54.7 us (level)
  no operation moved by 1% of the time
where the time goes in v5:
time: 54.7 us; the launch traced here: 54.5 us
  Pallas kernels  53.9 us (99%)
  between operations  0.64 us (1%)
    pallas_call x1, Pallas kernels, shards(): pl.pallas_call(functools.partial(move_kernel, nx, nz, nt), out_shape=(plt...  52.8 us

profile of v5, /device:TPU:1, one launch (start us, length us, event | category | flops | bytes accessed | tf_op | source)
XLA Modules:
  0.0 54.5 jit_solution(3238501407122856863)
XLA Ops:
  0.6 52.8 %shard_map.86 = (bf16[1,4,512]{2,1,0:T(4,128)(2,1)S(1)}, bf16[1,4,2,512,128]{4,3,2,1,0:T(8,128)(2,1)S(1)}) custom-call(s32[64]{0:T(128)} %dest_hbm.1, s32[64]{0:T(128)} %len_hbm.1, bf16[1,2,512]{2,1,0:T(2,128)(2,1)} %q_hbm.1, bf16[1,2,2,512,128]{4,3,2,1,0:T(8,128)(2,1)} %kv_hbm.1, bf16[1,2,2,128]{3,2,1,0:T(2,128)(2,1)} %fresh_hbm.1, ...), custom_call_target="tpu_custom_call" | custom-call | tf_op jit(solution)/shard_map/pallas_call | solution.py:303
  53.5 1.0 %shard_map.87 = (bf16[1,4,512]{2,1,0:T(4,128)(2,1)}, bf16[1,4,2,512,128]{4,3,2,1,0:T(8,128)(2,1)}) custom-call(bf16[1,4,512]{2,1,0:T(4,128)(2,1)S(1)} %get-tuple-element.4.handed, bf16[1,4,2,512,128]{4,3,2,1,0:T(8,128)(2,1)S(1)} %get-tuple-element.5.moved), custom_call_target="tpu_custom_call" | custom-call | tf_op jit(solution)/shard_map/pallas_call | solution.py:332

commit v6 on v5

--- a/solution.py
+++ b/solution.py
@@ -17,8 +17,8 @@
     dest_hbm, len_hbm, q_hbm, kv_hbm, fresh_hbm, res_hbm, w_hbm,
     handed_ref, cache_ref,
     dest_ref, len_ref, q_ref, fresh_ref, res_ref, row_of, row_of_ref,
-    kv, w, got_k, got_v, put_k, put_v, part, red, lay_own, lay,
-    in_sem, small_sem, row_sem, w_sem, own_sem, sent_sem, k1_sem, v1_sem, k2_sem, v2_sem, red_sent, red_sem, layz_sent, layx_sent, layz_sem, layx_sem,
+    kv, w, got, put, part, red, lay_own, lay,
+    in_sem, small_sem, row_sem, w_sem, own_sem, sent_sem, hop1_sem, hop2_sem, red_sent, red_sem, layz_sent, layx_sent, layz_sem, layx_sem,
 ):
     groups = nx * nz
     ctx = kv.shape[2]
@@ -30,17 +30,17 @@
     x = lax.div(g, nz)
     z = lax.rem(g, nz)
 
-    load_kv = [pltpu.make_async_copy(kv_hbm.at[0, :, c], kv.at[:, c], in_sem.at[c]) for c in range(2)]
-    for load in load_kv:
-        load.start()
+    load_kv = pltpu.make_async_copy(kv_hbm.at[0], kv, in_sem)
+    load_kv.start()
     small = [
         pltpu.make_async_copy(src, dst, small_sem.at[i])
         for i, (src, dst) in enumerate(
             ((len_hbm, len_ref), (fresh_hbm, fresh_ref), (q_hbm, q_ref), (dest_hbm, dest_ref), (res_hbm, res_ref))
         )
     ]
-    for load in small:
-        load.start()
+    load_len, load_fresh, *load_rest = small
+    load_len.start()
+    load_fresh.start()
 
     barrier = pltpu.get_barrier_semaphore()
 
@@ -62,7 +62,11 @@
     lax.fori_loop(1, nt, greet_tensor, 0)
     lax.fori_loop(0, nz, greet_section, 0)
 
-    load_len, load_fresh, *load_rest = small
+    for load in load_rest:
+        load.start()
+    load_w = pltpu.make_async_copy(w_hbm.at[0], w, w_sem)
+    load_w.start()
+
     load_len.wait()
     load_fresh.wait()
     len0 = len_ref[2 * g]
@@ -70,17 +74,14 @@
     pos = lax.broadcasted_iota(jnp.int32, (ctx, HD), 0)
     mine = pl.ds(pl.multiple_of(span * g, span), span)
 
-    def append(c, got):
-        load_kv[c].wait()
-        for r, n in ((0, len0), (1, len1)):
+    load_kv.wait()
+    for r, n in ((0, len0), (1, len1)):
+        for c in range(2):
             token = jnp.broadcast_to(fresh_ref[0, r, c : c + 1, :].astype(jnp.float32), (ctx, HD))
             kv[r, c] = jnp.where(pos == n, token, kv[r, c].astype(jnp.float32)).astype(jnp.bfloat16)
-            got[2 * g + r] = kv[r, c, mine, :]
-        got[rows] = jnp.zeros((span, HD), jnp.bfloat16)
-
-    append(0, got_k)
-    load_w = pltpu.make_async_copy(w_hbm.at[0], w, w_sem)
-    load_w.start()
+            got[2 * g + r, c] = kv[r, c, mine, :]
+    got[rows] = jnp.zeros((2, span, HD), jnp.bfloat16)
+
     pl.semaphore_wait(barrier, groups - 1 + nt - 1 + nz)
 
     z_offsets = [o for m in range(nz // 2 - 1, 0, -1) for o in (m, nz - m)]
@@ -103,22 +104,17 @@
 
         lax.fori_loop(low, high, window, 0)
 
-    def hop1(c, dst, sem, low, high):
-        def send(d):
-            pltpu.make_async_remote_copy(
-                src_ref=kv.at[:, c, pl.ds(pl.multiple_of(span * d, span), span), :],
-                dst_ref=dst.at[pl.ds(2 * g, 2)],
-                send_sem=sent_sem.at[c],
-                recv_sem=sem,
-                device_id={"group": d},
-                device_id_type=MESH,
-            ).start()
-
-        for_partners(low, high, send)
-
-    hop1(0, got_k, k1_sem, 0, nx)
-    append(1, got_v)
-    hop1(1, got_v, v1_sem, 0, nx)
+    def hop1(d):
+        pltpu.make_async_remote_copy(
+            src_ref=kv.at[:, :, pl.ds(pl.multiple_of(span * d, span), span), :],
+            dst_ref=got.at[pl.ds(2 * g, 2)],
+            send_sem=sent_sem.at[0],
+            recv_sem=hop1_sem,
+            device_id={"group": d},
+            device_id_type=MESH,
+        ).start()
+
+    for_partners(0, nx, hop1)
 
     for load in load_rest:
         load.wait()
@@ -162,26 +158,20 @@
     def wait_bytes(ref, sem):
         pltpu.make_async_copy(ref, ref, sem).wait()
 
-    def hop2(c, got, put, sem, low, high):
-        def copy_slots(d):
-            for slot in range(4):
-                put[4 * d + slot] = got[row_of_ref[0, 4 * d + slot]]
-
-        def send(d):
-            copy_slots(d)
-            pltpu.make_async_remote_copy(
-                src_ref=put.at[pl.ds(4 * d, 4)],
-                dst_ref=cache_ref.at[0, :, c, mine, :],
-                send_sem=sent_sem.at[2 + c],
-                recv_sem=sem,
-                device_id={"group": d},
-                device_id_type=MESH,
-            ).start()
-
-        for_partners(low, high, send)
-        if high == nx:
-            copy_slots(g)
-            pltpu.make_async_copy(put.at[pl.ds(4 * g, 4)], cache_ref.at[0, :, c, mine, :], own_sem.at[c]).start()
+    def copy_slots(d):
+        for slot in range(4):
+            put[4 * d + slot] = got[row_of_ref[0, 4 * d + slot]]
+
+    def hop2(d):
+        copy_slots(d)
+        pltpu.make_async_remote_copy(
+            src_ref=put.at[pl.ds(4 * d, 4)],
+            dst_ref=cache_ref.at[0, :, :, mine, :],
+            send_sem=sent_sem.at[1],
+            recv_sem=hop2_sem,
+            device_id={"group": d},
+            device_id_type=MESH,
+        ).start()
 
     width = res_ref.shape[2]
     load_w.wait()
@@ -212,8 +202,8 @@
     red[t] = part[t]
 
     load_row_of.wait()
-    wait_bytes(got_k.at[pl.ds(0, rows - 2)], k1_sem)
-    hop2(0, got_k, put_k, k2_sem, 0, nx // 2)
+    wait_bytes(got.at[pl.ds(0, rows - 2)], hop1_sem)
+    for_partners(0, nx // 4, hop2)
 
     wait_bytes(red.at[pl.ds(0, nt - 1)], red_sem)
     total = red[0]
@@ -235,7 +225,7 @@
 
     lax.fori_loop(0, nz, hand, 0)
 
-    hop2(0, got_k, put_k, k2_sem, nx // 2, nx)
+    for_partners(nx // 4, nx // 2, hop2)
 
     ring = pl.ds(nz * x, nz)
     wait_bytes(lay.at[pl.ds(0, nz)], layz_sem)
@@ -253,8 +243,10 @@
 
     lax.fori_loop(1, nx, spread, 0)
 
-    wait_bytes(got_v.at[pl.ds(0, rows - 2)], v1_sem)
-    hop2(1, got_v, put_v, v2_sem, 0, nx)
+    for_partners(nx // 2, nx, hop2)
+    copy_slots(g)
+    own = pltpu.make_async_copy(put.at[pl.ds(4 * g, 4)], cache_ref.at[0, :, :, mine, :], own_sem)
+    own.start()
 
     wait_bytes(lay.at[pl.ds(0, nz * (nx - 1))], layx_sem)
     out_rows = []
@@ -267,12 +259,10 @@
     wait_bytes(part.at[pl.ds(0, nt - 1)], red_sent)
     wait_bytes(lay.at[pl.ds(0, nz)], layz_sent)
     wait_bytes(lay.at[pl.ds(0, nz * (nx - 1))], layx_sent)
-    wait_bytes(got_k.at[pl.ds(0, rows - 2)], sent_sem.at[0])
-    wait_bytes(got_v.at[pl.ds(0, rows - 2)], sent_sem.at[1])
-    for c, put, sem in ((0, put_k, k2_sem), (1, put_v, v2_sem)):
-        pltpu.make_async_copy(put.at[pl.ds(4 * g, 4)], cache_ref.at[0, :, c, mine, :], own_sem.at[c]).wait()
-        wait_bytes(put.at[pl.ds(0, 4 * (groups - 1))], sent_sem.at[2 + c])
-        wait_bytes(put.at[pl.ds(0, 4 * (groups - 1))], sem)
+    wait_bytes(got.at[pl.ds(0, rows - 2)], sent_sem.at[0])
+    own.wait()
+    wait_bytes(put.at[pl.ds(0, 4 * (groups - 1))], sent_sem.at[1])
+    wait_bytes(put.at[pl.ds(0, 4 * (groups - 1))], hop2_sem)
 
 
 def write_kernel(handed, moved, handed_hbm, moved_hbm, sem):
@@ -315,15 +305,13 @@
             pltpu.SMEM((8, cells), jnp.int32),
             pltpu.VMEM((2, 2, ctx, HD), bf),
             pltpu.VMEM(out_weight.shape[1:], bf),
-            pltpu.VMEM((rows + 1, span, HD), bf),
-            pltpu.VMEM((rows + 1, span, HD), bf),
-            pltpu.VMEM((cells, span, HD), bf),
-            pltpu.VMEM((cells, span, HD), bf),
+            pltpu.VMEM((rows + 1, 2, span, HD), bf),
+            pltpu.VMEM((cells, 2, span, HD), bf),
             pltpu.VMEM((nt, 2, width), f32),
             pltpu.VMEM((nt, 2, width), f32),
             pltpu.VMEM((2, width), bf),
             pltpu.VMEM((groups, 2, width), bf),
-            dma((2,)), dma((5,)), dma, dma, dma((2,)), dma((4,)), dma, dma, dma, dma, dma, dma, dma, dma, dma, dma,
+            dma, dma((5,)), dma, dma, dma, dma((2,)), dma, dma, dma, dma, dma, dma, dma, dma,
         ],
         compiler_params=pltpu.CompilerParams(
             collective_id=0, has_side_effects=True, vmem_limit_bytes=60 * 1024 * 1024

time: 54.7 us -> 56.6 us (1.035)
  Pallas kernels: 53.9 us -> 55.8 us
    pallas_call x1, Pallas kernels: 52.8 us -> 54.8 us  [shards(): pl.pallas_call(functools.partial(move_kernel, nx, nz, nt), out_shape=(plt...]
where the time goes in v6:
time: 56.6 us; the launch traced here: 56.5 us
  Pallas kernels  55.8 us (99%)
  between operations  0.64 us (1%)
    pallas_call x1, Pallas kernels, shards(): pl.pallas_call(functools.partial(move_kernel, nx, nz, nt), out_shape=(plt...  54.8 us

profile of v6, /device:TPU:1, one launch (start us, length us, event | category | flops | bytes accessed | tf_op | source)
XLA Modules:
  0.0 56.5 jit_solution(6514675863994385671)
XLA Ops:
  0.6 54.8 %shard_map.86 = (bf16[1,4,512]{2,1,0:T(4,128)(2,1)S(1)}, bf16[1,4,2,512,128]{4,3,2,1,0:T(8,128)(2,1)S(1)}) custom-call(s32[64]{0:T(128)} %dest_hbm.1, s32[64]{0:T(128)} %len_hbm.1, bf16[1,2,512]{2,1,0:T(2,128)(2,1)} %q_hbm.1, bf16[1,2,2,512,128]{4,3,2,1,0:T(8,128)(2,1)} %kv_hbm.1, bf16[1,2,2,128]{3,2,1,0:T(2,128)(2,1)} %fresh_hbm.1, ...), custom_call_target="tpu_custom_call" | custom-call | tf_op jit(solution)/shard_map/pallas_call | solution.py:293
  55.4 1.0 %shard_map.87 = (bf16[1,4,512]{2,1,0:T(4,128)(2,1)}, bf16[1,4,2,512,128]{4,3,2,1,0:T(8,128)(2,1)}) custom-call(bf16[1,4,512]{2,1,0:T(4,128)(2,1)S(1)} %get-tuple-element.4.handed, bf16[1,4,2,512,128]{4,3,2,1,0:T(8,128)(2,1)S(1)} %get-tuple-element.5.moved), custom_call_target="tpu_custom_call" | custom-call | tf_op jit(solution)/shard_map/pallas_call | solution.py:320

commit v7 on v5

--- a/solution.py
+++ b/solution.py
@@ -31,16 +31,16 @@
     z = lax.rem(g, nz)
 
     load_kv = [pltpu.make_async_copy(kv_hbm.at[0, :, c], kv.at[:, c], in_sem.at[c]) for c in range(2)]
-    for load in load_kv:
-        load.start()
+    load_kv[0].start()
     small = [
         pltpu.make_async_copy(src, dst, small_sem.at[i])
         for i, (src, dst) in enumerate(
             ((len_hbm, len_ref), (fresh_hbm, fresh_ref), (q_hbm, q_ref), (dest_hbm, dest_ref), (res_hbm, res_ref))
         )
     ]
-    for load in small:
-        load.start()
+    load_len, load_fresh, *load_rest = small
+    load_len.start()
+    load_fresh.start()
 
     barrier = pltpu.get_barrier_semaphore()
 
@@ -58,11 +58,15 @@
         )
         return carry
 
-    lax.fori_loop(1, groups, greet_group, 0)
-    lax.fori_loop(1, nt, greet_tensor, 0)
-    lax.fori_loop(0, nz, greet_section, 0)
-
-    load_len, load_fresh, *load_rest = small
+    lax.fori_loop(1, groups, greet_group, 0, unroll=True)
+    lax.fori_loop(1, nt, greet_tensor, 0, unroll=True)
+    lax.fori_loop(0, nz, greet_section, 0, unroll=True)
+
+    for load in (load_kv[1], *load_rest):
+        load.start()
+    load_w = pltpu.make_async_copy(w_hbm.at[0], w, w_sem)
+    load_w.start()
+
     load_len.wait()
     load_fresh.wait()
     len0 = len_ref[2 * g]
@@ -79,8 +83,6 @@
         got[rows] = jnp.zeros((span, HD), jnp.bfloat16)
 
     append(0, got_k)
-    load_w = pltpu.make_async_copy(w_hbm.at[0], w, w_sem)
-    load_w.start()
     pl.semaphore_wait(barrier, groups - 1 + nt - 1 + nz)
 
     z_offsets = [o for m in range(nz // 2 - 1, 0, -1) for o in (m, nz - m)]
@@ -89,19 +91,20 @@
 
     way = 1 - 2 * s
 
-    z_partners = [lax.rem(z + way * dz + nz, nz) for dz in z_offsets]
+    later = z_offsets[nz // 2 :] + z_offsets[: nz // 2]
+    z_partners = [lax.rem(z + jnp.where(s == 0, dz, nz - dz_later), nz) for dz, dz_later in zip(z_offsets, later)]
 
     def for_partners(low, high, send):
         def window(v, carry):
-            for j, dz in enumerate(z_offsets):
+            for j in range(nz):
                 d = lax.rem(x + way * (j + v) + nx * nz, nx) * nz + z_partners[j]
-                if dz == 0:
-                    pl.when(lax.rem(j + v, nx) != 0)(functools.partial(send, d))
+                if 0 in (z_offsets[j], later[j]):
+                    pl.when(d != g)(functools.partial(send, d))
                 else:
                     send(d)
             return carry
 
-        lax.fori_loop(low, high, window, 0)
+        lax.fori_loop(low, high, window, 0, unroll=True)
 
     def hop1(c, dst, sem, low, high):
         def send(d):
@@ -233,7 +236,7 @@
         ).start()
         return carry
 
-    lax.fori_loop(0, nz, hand, 0)
+    lax.fori_loop(0, nz, hand, 0, unroll=True)
 
     hop2(0, got_k, put_k, k2_sem, nx // 2, nx)
 
@@ -251,7 +254,7 @@
         ).start()
         return carry
 
-    lax.fori_loop(1, nx, spread, 0)
+    lax.fori_loop(1, nx, spread, 0, unroll=True)
 
     wait_bytes(got_v.at[pl.ds(0, rows - 2)], v1_sem)
     hop2(1, got_v, put_v, v2_sem, 0, nx)

time: 54.7 us -> 53.9 us (0.985)
  Pallas kernels: 53.9 us -> 53.1 us
    pallas_call x1, Pallas kernels: 52.8 us -> 52.1 us  [shards(): pl.pallas_call(functools.partial(move_kernel, nx, nz, nt), out_shape=(plt...]
where the time goes in v7:
time: 53.9 us; the launch traced here: 53.8 us
  Pallas kernels  53.1 us (99%)
  between operations  0.64 us (1%)
    pallas_call x1, Pallas kernels, shards(): pl.pallas_call(functools.partial(move_kernel, nx, nz, nt), out_shape=(plt...  52.1 us

profile of v7, /device:TPU:1, one launch (start us, length us, event | category | flops | bytes accessed | tf_op | source)
XLA Modules:
  0.0 53.8 jit_solution(7278384578854508727)
XLA Ops:
  0.6 52.1 %shard_map.86 = (bf16[1,4,512]{2,1,0:T(4,128)(2,1)S(1)}, bf16[1,4,2,512,128]{4,3,2,1,0:T(8,128)(2,1)S(1)}) custom-call(s32[64]{0:T(128)} %dest_hbm.1, s32[64]{0:T(128)} %len_hbm.1, bf16[1,2,512]{2,1,0:T(2,128)(2,1)} %q_hbm.1, bf16[1,2,2,512,128]{4,3,2,1,0:T(8,128)(2,1)} %kv_hbm.1, bf16[1,2,2,128]{3,2,1,0:T(2,128)(2,1)} %fresh_hbm.1, ...), custom_call_target="tpu_custom_call" | custom-call | tf_op jit(solution)/shard_map/pallas_call | solution.py:306
  52.7 1.0 %shard_map.87 = (bf16[1,4,512]{2,1,0:T(4,128)(2,1)}, bf16[1,4,2,512,128]{4,3,2,1,0:T(8,128)(2,1)}) custom-call(bf16[1,4,512]{2,1,0:T(4,128)(2,1)S(1)} %get-tuple-element.4.handed, bf16[1,4,2,512,128]{4,3,2,1,0:T(8,128)(2,1)S(1)} %get-tuple-element.5.moved), custom_call_target="tpu_custom_call" | custom-call | tf_op jit(solution)/shard_map/pallas_call | solution.py:335

commit v8 on v7

--- a/solution.py
+++ b/solution.py
@@ -91,14 +91,21 @@
 
     way = 1 - 2 * s
 
-    later = z_offsets[nz // 2 :] + z_offsets[: nz // 2]
-    z_partners = [lax.rem(z + jnp.where(s == 0, dz, nz - dz_later), nz) for dz, dz_later in zip(z_offsets, later)]
+    odd = lax.rem(x, 2)
+    z_partners = []
+    may_be_own = []
+    for j in range(nz):
+        even_0, odd_0, even_1, odd_1 = (z_offsets[(j + i * nz // 4) % nz] for i in range(4))
+        ahead = jnp.where(odd == 0, even_0, odd_0)
+        behind = nz - jnp.where(odd == 0, even_1, odd_1)
+        z_partners.append(lax.rem(z + jnp.where(s == 0, ahead, behind), nz))
+        may_be_own.append(0 in (even_0, odd_0, even_1, odd_1))
 
     def for_partners(low, high, send):
         def window(v, carry):
             for j in range(nz):
                 d = lax.rem(x + way * (j + v) + nx * nz, nx) * nz + z_partners[j]
-                if 0 in (z_offsets[j], later[j]):
+                if may_be_own[j]:
                     pl.when(d != g)(functools.partial(send, d))
                 else:
                     send(d)

time: 53.9 us -> 54.2 us (level)
  no operation moved by 1% of the time
where the time goes in v8:
time: 54.2 us; the launch traced here: 54.1 us
  Pallas kernels  53.4 us (99%)
  between operations  0.64 us (1%)
    pallas_call x1, Pallas kernels, shards(): pl.pallas_call(functools.partial(move_kernel, nx, nz, nt), out_shape=(plt...  52.4 us

profile of v8, /device:TPU:1, one launch (start us, length us, event | category | flops | bytes accessed | tf_op | source)
XLA Modules:
  0.0 54.1 jit_solution(1635611655416422895)
XLA Ops:
  0.6 52.4 %shard_map.86 = (bf16[1,4,512]{2,1,0:T(4,128)(2,1)S(1)}, bf16[1,4,2,512,128]{4,3,2,1,0:T(8,128)(2,1)S(1)}) custom-call(s32[64]{0:T(128)} %dest_hbm.1, s32[64]{0:T(128)} %len_hbm.1, bf16[1,2,512]{2,1,0:T(2,128)(2,1)} %q_hbm.1, bf16[1,2,2,512,128]{4,3,2,1,0:T(8,128)(2,1)} %kv_hbm.1, bf16[1,2,2,128]{3,2,1,0:T(2,128)(2,1)} %fresh_hbm.1, ...), custom_call_target="tpu_custom_call" | custom-call | tf_op jit(solution)/shard_map/pallas_call | solution.py:313
  53.0 1.0 %shard_map.87 = (bf16[1,4,512]{2,1,0:T(4,128)(2,1)}, bf16[1,4,2,512,128]{4,3,2,1,0:T(8,128)(2,1)}) custom-call(bf16[1,4,512]{2,1,0:T(4,128)(2,1)S(1)} %get-tuple-element.4.handed, bf16[1,4,2,512,128]{4,3,2,1,0:T(8,128)(2,1)S(1)} %get-tuple-element.5.moved), custom_call_target="tpu_custom_call" | custom-call | tf_op jit(solution)/shard_map/pallas_call | solution.py:342

commit v9 on v7

--- a/solution.py
+++ b/solution.py
@@ -240,6 +240,9 @@
 
     hop2(0, got_k, put_k, k2_sem, nx // 2, nx)
 
+    wait_bytes(got_v.at[pl.ds(0, rows - 2)], v1_sem)
+    hop2(1, got_v, put_v, v2_sem, 0, nx // 2)
+
     ring = pl.ds(nz * x, nz)
     wait_bytes(lay.at[pl.ds(0, nz)], layz_sem)
 
@@ -256,8 +259,7 @@
 
     lax.fori_loop(1, nx, spread, 0, unroll=True)
 
-    wait_bytes(got_v.at[pl.ds(0, rows - 2)], v1_sem)
-    hop2(1, got_v, put_v, v2_sem, 0, nx)
+    hop2(1, got_v, put_v, v2_sem, nx // 2, nx)
 
     wait_bytes(lay.at[pl.ds(0, nz * (nx - 1))], layx_sem)
     out_rows = []

time: 53.9 us -> 53.9 us (level)
  the two profiles are of different devices: /device:TPU:1 before, /device:TPU:8 now
where the time goes in v9:
time: 53.9 us; the launch traced here: 53.7 us
  Pallas kernels  53.1 us (99%)
  between operations  0.64 us (1%)
    pallas_call x1, Pallas kernels, shards(): pl.pallas_call(functools.partial(move_kernel, nx, nz, nt), out_shape=(plt...  52.1 us

profile of v9, /device:TPU:8, one launch (start us, length us, event | category | flops | bytes accessed | tf_op | source)
XLA Modules:
  0.0 53.7 jit_solution(17724610961225890268)
XLA Ops:
  0.6 52.1 %shard_map.86 = (bf16[1,4,512]{2,1,0:T(4,128)(2,1)S(1)}, bf16[1,4,2,512,128]{4,3,2,1,0:T(8,128)(2,1)S(1)}) custom-call(s32[64]{0:T(128)} %dest_hbm.1, s32[64]{0:T(128)} %len_hbm.1, bf16[1,2,512]{2,1,0:T(2,128)(2,1)} %q_hbm.1, bf16[1,2,2,512,128]{4,3,2,1,0:T(8,128)(2,1)} %kv_hbm.1, bf16[1,2,2,128]{3,2,1,0:T(2,128)(2,1)} %fresh_hbm.1, ...), custom_call_target="tpu_custom_call" | custom-call | tf_op jit(solution)/shard_map/pallas_call | solution.py:308
  52.7 1.0 %shard_map.87 = (bf16[1,4,512]{2,1,0:T(4,128)(2,1)}, bf16[1,4,2,512,128]{4,3,2,1,0:T(8,128)(2,1)}) custom-call(bf16[1,4,512]{2,1,0:T(4,128)(2,1)S(1)} %get-tuple-element.4.handed, bf16[1,4,2,512,128]{4,3,2,1,0:T(8,128)(2,1)S(1)} %get-tuple-element.5.moved), custom_call_target="tpu_custom_call" | custom-call | tf_op jit(solution)/shard_map/pallas_call | solution.py:337

commit v10 on v9

--- a/solution.py
+++ b/solution.py
@@ -216,7 +216,7 @@
 
     load_row_of.wait()
     wait_bytes(got_k.at[pl.ds(0, rows - 2)], k1_sem)
-    hop2(0, got_k, put_k, k2_sem, 0, nx // 2)
+    hop2(0, got_k, put_k, k2_sem, 0, nx)
 
     wait_bytes(red.at[pl.ds(0, nt - 1)], red_sem)
     total = red[0]
@@ -238,7 +238,6 @@
 
     lax.fori_loop(0, nz, hand, 0, unroll=True)
 
-    hop2(0, got_k, put_k, k2_sem, nx // 2, nx)
 
     wait_bytes(got_v.at[pl.ds(0, rows - 2)], v1_sem)
     hop2(1, got_v, put_v, v2_sem, 0, nx // 2)

time: 53.9 us -> 53.9 us (level)
  the two profiles are of different devices: /device:TPU:8 before, /device:TPU:1 now
where the time goes in v10:
time: 53.9 us; the launch traced here: 53.5 us
  Pallas kernels  52.8 us (98%)
  between operations  0.64 us (1%)
    pallas_call x1, Pallas kernels, shards(): pl.pallas_call(functools.partial(move_kernel, nx, nz, nt), out_shape=(plt...  51.8 us

profile of v10, /device:TPU:1, one launch (start us, length us, event | category | flops | bytes accessed | tf_op | source)
XLA Modules:
  0.0 53.5 jit_solution(341430220308401402)
XLA Ops:
  0.6 51.8 %shard_map.86 = (bf16[1,4,512]{2,1,0:T(4,128)(2,1)S(1)}, bf16[1,4,2,512,128]{4,3,2,1,0:T(8,128)(2,1)S(1)}) custom-call(s32[64]{0:T(128)} %dest_hbm.1, s32[64]{0:T(128)} %len_hbm.1, bf16[1,2,512]{2,1,0:T(2,128)(2,1)} %q_hbm.1, bf16[1,2,2,512,128]{4,3,2,1,0:T(8,128)(2,1)} %kv_hbm.1, bf16[1,2,2,128]{3,2,1,0:T(2,128)(2,1)} %fresh_hbm.1, ...), custom_call_target="tpu_custom_call" | custom-call | tf_op jit(solution)/shard_map/pallas_call | solution.py:307
  52.4 1.0 %shard_map.87 = (bf16[1,4,512]{2,1,0:T(4,128)(2,1)}, bf16[1,4,2,512,128]{4,3,2,1,0:T(8,128)(2,1)}) custom-call(bf16[1,4,512]{2,1,0:T(4,128)(2,1)S(1)} %get-tuple-element.4.handed, bf16[1,4,2,512,128]{4,3,2,1,0:T(8,128)(2,1)S(1)} %get-tuple-element.5.moved), custom_call_target="tpu_custom_call" | custom-call | tf_op jit(solution)/shard_map/pallas_call | solution.py:336
